TPU v7x, 32 devices: a whole 2x2x4 slice. The times are simulated.
32 devices in a mesh: shard: 4 (over y, core), ctx: 4 (over z), tp: 2 (over x).
Axes of the slice: x: 2, y: 2, z: 4, core: 2. Of those that a mesh axis runs over, the one named last changes fastest.
Arguments:
- stream: bfloat16 [8, 1024, 2048], P('shard', 'ctx', 'tp'), may hold values from -14 to 14
- norm_gain: float32 [2048], replicated, may hold values from 0.5 to 1.5
- in_weight: bfloat16 [2, 2048, 2, 4096], P(None, 'shard', None, 'tp'), may hold values from -0.125 to 0.125
- select_weight: bfloat16 [2, 160, 4096], P(None, 'shard', 'tp'), may hold values from -0.09375 to 0.09375
- delta_weight: bfloat16 [2, 128, 4096], P(None, 'shard', 'tp'), may hold values from -0.5 to 0.5
- delta_bias: float32 [2, 4096], P(None, 'tp'), may hold values from -6.9 to -2.3
- out_weight: bfloat16 [4096, 2048], P('tp', 'shard'), may hold values from -0.375 to 0.375
- filter_weight: float32 [4, 4096], P(None, 'tp'), may hold values from -3 to 3
- filter_bias: float32 [4096], P('tp'), may hold values from -0.5 to 0.5
- decay_log: float32 [16, 4096], P(None, 'tp'), may hold values from -1 to 2.5
- skip_gain: float32 [4096], P('tp'), may hold values from 0.5 to 1.5
- segments: int32 [8, 1024], P('shard'), may hold values from 0 to 3, never falling along the last dimension, each value on 1 to 800 neighbouring positions
- modality: int32 [8, 1024], P('shard', 'ctx'), may hold values from 0 to 1
- valid: int32 [8, 1024], P('shard', 'ctx'), may hold values 0 or 1
- upstream: bfloat16 [8, 1024, 2048], P('shard', 'ctx', 'tp'), may hold values from -6 to 6
Outputs:
- output: bfloat16 [8, 1024, 2048], P('shard', 'ctx', 'tp')
- stream_gradient: bfloat16 [8, 1024, 2048], P('shard', 'ctx', 'tp')
- gain_gradient: float32 [2048], P('tp')
- in_gradient: float32 [2, 2048, 2, 4096], P(None, ('shard', 'ctx'), None, 'tp')
- select_gradient: float32 [2, 160, 4096], P(None, ('shard', 'ctx'), 'tp')
- delta_gradient: float32 [2, 128, 4096], P(None, ('shard', 'ctx'), 'tp')
- bias_gradient: float32 [2, 4096], P(None, 'tp')
- out_gradient: float32 [4096, 2048], P('tp', ('shard', 'ctx'))
- filter_gradient: float32 [4, 4096], P(None, 'tp')
- offset_gradient: float32 [4096], P('tp')
- decay_gradient: float32 [16, 4096], P(None, 'tp')
- skip_gradient: float32 [4096], P('tp')
- stream_rms: float32 [], replicated
- mixer_rms: float32 [], replicated
Inputs may be any that keep to these rules, and one draw needn't show every extreme that they name: `segments`: in each sequence segment numbers start at 0 and never fall; each document covers 1 to 800 positions.
All inputs are finite; a program needn't handle non-finite values. No bound on the sum of `valid` on one device may be relied on, other than what follows from the above.
Results may differ from a plain program's by a relative error of at most 0.012.
Values may be sent and summed in bfloat16 or wider, within the bound.
A program may use at most 384 MiB of HBM per device.

v0:
```python
import functools
import jax
import jax.numpy as jnp
from jax import lax
from jax.experimental import pallas as pl
from jax.experimental.pallas import tpu as pltpu

LOG2E = 1.4426950408889634
VMEM_LIMIT = 60 * 1024 * 1024


def sigmoid(value):
    return 1.0 / (1.0 + jnp.exp(-value))


def softplus(value):
    return jnp.maximum(value, 0.0) + jnp.log1p(jnp.exp(-jnp.abs(value)))


def stage_rows(raw_ref, conv_ref, gate_ref, gg_ref, delta_s, conv_s, g_s, groups):
    def step(block, _):
        top = pl.multiple_of(block * 16, 16)
        for group in range(groups):
            lanes = slice(group * 128, group * 128 + 128)
            delta = softplus(raw_ref[pl.ds(top, 16), lanes])
            conv = conv_ref[pl.ds(top, 16), lanes].astype(jnp.float32)
            gate = gate_ref[pl.ds(top, 16), lanes]
            g_mixed = gg_ref[pl.ds(top, 16), lanes] * (gate * sigmoid(gate))
            for part in range(2):
                rows = pl.ds(pl.multiple_of(((block * 2 + part) * groups + group) * 8, 8), 8)
                eight = slice(part * 8, part * 8 + 8)
                delta_s[rows, :] = delta[eight]
                conv_s[rows, :] = conv[eight]
                g_s[rows, :] = g_mixed[eight]
        return 0

    lax.fori_loop(0, raw_ref.shape[0] // 16, step, 0)


def ends_kernel(groups, states, split, raw_ref, conv_ref, gate_ref, gg_ref, a_ref, b_ref, c_ref,
                cut_ref, h_ref, p_ref, l_ref, delta_s, conv_s, g_s):
    tokens = raw_ref.shape[0]
    first = pl.program_id(0) * tokens
    stage_rows(raw_ref, conv_ref, gate_ref, gg_ref, delta_s, conv_s, g_s, groups)
    for low in range(0, states, split):
        names = range(low, low + split)

        def eight_tokens(tile, carry):
            h, p, l = (list(part) for part in carry)
            for i in range(8):
                rows = pl.ds(tile * (groups * 8) + i, groups, stride=8)
                delta = delta_s[rows, :]
                signal = delta * conv_s[rows, :]
                g = g_s[rows, :]
                token = first + tile * 8 + i
                reach = delta + cut_ref[token]
                for k, n in enumerate(names):
                    decay = jnp.exp2(reach * a_ref[n])
                    h[k] = decay * h[k] + signal * b_ref[token * states + n]
                    p[k] = decay * p[k]
                    l[k] = l[k] + p[k] * (g * c_ref[token * states + n])
            return tuple(h), tuple(p), tuple(l)

        zero = tuple(jnp.zeros((groups, 128), jnp.float32) for _ in names)
        one = tuple(jnp.ones((groups, 128), jnp.float32) for _ in names)
        h, p, l = lax.fori_loop(0, tokens // 8, eight_tokens, (zero, one, zero))
        for k, n in enumerate(names):
            h_ref[n], p_ref[n], l_ref[n] = h[k], p[k], l[k]


def scan_kernel(groups, states, fsplit, bsplit, raw_ref, conv_ref, gate_ref, gg_ref, skip_ref, a_ref, h0_ref,
                q0_ref, b_ref, c_ref, cut_ref, gated_ref, ggate_ref, graw_ref, gconv_ref,
                ga_ref, gb_ref, gc_ref, gskip_ref, delta_s, conv_s, g_s, y_s, gs_s, h_s):
    tokens = raw_ref.shape[0]
    tiles = tokens // 8
    first = pl.program_id(0) * tokens
    stage_rows(raw_ref, conv_ref, gate_ref, gg_ref, delta_s, conv_s, g_s, groups)
    lane = lax.broadcasted_iota(jnp.int32, (groups, 128), 1)

    def split_sum(total, names, values, i):
        for n, value in zip(names, values):
            total = jnp.where(lane == i * states + n, jnp.sum(value, axis=1, keepdims=True), total)
        return total

    for low in range(0, states, fsplit):
        names = range(low, low + fsplit)

        def forward(tile, h):
            h = list(h)
            gc = jnp.zeros((groups, 128), jnp.float32) if low == 0 else gc_ref[tile]
            for i in range(8):
                rows = pl.ds(tile * (groups * 8) + i, groups, stride=8)
                delta = delta_s[rows, :]
                signal = delta * conv_s[rows, :]
                g = g_s[rows, :]
                token = tile * 8 + i
                at = (first + token) * states
                reach = delta + cut_ref[first + token]
                y = None
                parts = []
                for k, n in enumerate(names):
                    h_s[token, n] = h[k]
                    decay = jnp.exp2(reach * a_ref[n])
                    h[k] = decay * h[k] + signal * b_ref[at + n]
                    term = h[k] * c_ref[at + n]
                    y = term if y is None else y + term
                    parts.append(h[k] * g)
                gc = split_sum(gc, names, parts, i)
                y_s[rows, :] = y if low == 0 else y + y_s[rows, :]
            gc_ref[tile] = gc
            return tuple(h)

        lax.fori_loop(0, tiles, forward, tuple(h0_ref[n] for n in names))

    def between(block, total):
        top = pl.multiple_of(block * 16, 16)
        new = []
        for group in range(groups):
            lanes = slice(group * 128, group * 128 + 128)
            gate = gate_ref[pl.ds(top, 16), lanes]
            sig = sigmoid(gate)
            y, conv, g = (
                jnp.concatenate([ref[pl.ds(pl.multiple_of(((block * 2 + part) * groups + group) * 8, 8), 8), :]
                                 for part in range(2)], axis=0)
                for ref in (y_s, conv_s, g_s)
            )
            mixed = y + skip_ref[:, lanes] * conv
            gated_ref[pl.ds(top, 16), lanes] = (mixed * (gate * sig)).astype(jnp.bfloat16)
            g_gate = gg_ref[pl.ds(top, 16), lanes] * mixed * sig * (1.0 + gate * (1.0 - sig))
            ggate_ref[pl.ds(top, 16), lanes] = g_gate.astype(jnp.bfloat16)
            product = g * conv
            new.append(total[group] + product[:8] + product[8:])
        return tuple(new)

    sums = lax.fori_loop(0, tokens // 16, between,
                         tuple(jnp.zeros((8, 128), jnp.float32) for _ in range(groups)))
    for group in range(groups):
        gskip_ref[:, group * 128:group * 128 + 128] = sums[group]

    for low in range(0, states, bsplit):
        names = range(low, low + bsplit)

        def backward(step, carry):
            q, ga = (list(part) for part in carry)
            tile = tiles - 1 - step
            gb = jnp.zeros((groups, 128), jnp.float32) if low == 0 else gb_ref[tile]
            for i in reversed(range(8)):
                rows = pl.ds(tile * (groups * 8) + i, groups, stride=8)
                delta = delta_s[rows, :]
                conv = conv_s[rows, :]
                signal = delta * conv
                g = g_s[rows, :]
                token = tile * 8 + i
                at = (first + token) * states
                reach = delta + cut_ref[first + token]
                gd = gs = None
                parts = []
                for k, n in enumerate(names):
                    decay = jnp.exp2(reach * a_ref[n])
                    lam = q[k] + g * c_ref[at + n]
                    q[k] = decay * lam
                    w = q[k] * h_s[token, n]
                    ga[k] = ga[k] + w * delta
                    d_term = w * a_ref[n]
                    s_term = lam * b_ref[at + n]
                    gd = d_term if gd is None else gd + d_term
                    gs = s_term if gs is None else gs + s_term
                    parts.append(lam * signal)
                gb = split_sum(gb, names, parts, i)
                y_s[rows, :] = gd if low == 0 else gd + y_s[rows, :]
                gs_s[rows, :] = gs if low == 0 else gs + gs_s[rows, :]
            gb_ref[tile] = gb
            return tuple(q), tuple(ga)

        zero = tuple(jnp.zeros((groups, 128), jnp.float32) for _ in names)
        _, ga = lax.fori_loop(0, tiles, backward, (tuple(q0_ref[n] for n in names), zero))
        for k, n in enumerate(names):
            ga_ref[n] = ga[k]

    def after(block, _):
        top = pl.multiple_of(block * 16, 16)
        for group in range(groups):
            lanes = slice(group * 128, group * 128 + 128)
            raw = raw_ref[pl.ds(top, 16), lanes]
            gd, gs, conv, delta, g = (
                jnp.concatenate([ref[pl.ds(pl.multiple_of(((block * 2 + part) * groups + group) * 8, 8), 8), :]
                                 for part in range(2)], axis=0)
                for ref in (y_s, gs_s, conv_s, delta_s, g_s)
            )
            g_delta = gd * (1.0 / LOG2E) + conv * gs
            graw_ref[pl.ds(top, 16), lanes] = (g_delta * sigmoid(raw)).astype(jnp.bfloat16)
            gconv_ref[pl.ds(top, 16), lanes] = skip_ref[:, lanes] * g + delta * gs
        return 0

    lax.fori_loop(0, tokens // 16, after, 0)


def sizes(raw, seqs, states):
    rows, inner = raw.shape
    groups = min(8, inner // 128)
    return rows // seqs, inner // (groups * 128), groups


def state_form(value, blocks, groups):
    states = value.shape[0]
    return value.reshape(states, blocks, groups, 128).transpose(1, 0, 2, 3)


def from_state_form(value):
    blocks, states, groups, lanes = value.shape
    return value.transpose(1, 0, 2, 3).reshape(states, blocks * groups * lanes)


def token_spec(tokens, width):
    return pl.BlockSpec((tokens, width), lambda s, j: (s, j))


def state_spec(states, groups):
    return pl.BlockSpec((None, None, states, groups, 128), lambda s, j: (s, j, 0, 0, 0))


def scan_ends(raw, conv, gate, gg, a2, b, c, cut, seqs, split=16):
    blocks, states, groups, _ = a2.shape
    tokens, _, _ = sizes(raw, seqs, states)
    width = groups * 128
    smem = pl.BlockSpec(memory_space=pltpu.SMEM)
    out = jax.ShapeDtypeStruct((seqs, blocks, states, groups, 128), jnp.float32)
    elements = raw.size * states
    return pl.pallas_call(
        functools.partial(ends_kernel, groups, states, min(split, states)),
        grid=(seqs, blocks),
        in_specs=[token_spec(tokens, width)] * 4
        + [pl.BlockSpec((None, states, groups, 128), lambda s, j: (j, 0, 0, 0)), smem, smem, smem],
        out_specs=[state_spec(states, groups)] * 3,
        out_shape=[out] * 3,
        scratch_shapes=[pltpu.VMEM((tokens * groups, 128), jnp.float32)] * 3,
        compiler_params=pltpu.CompilerParams(vmem_limit_bytes=VMEM_LIMIT),
        cost_estimate=pl.CostEstimate(flops=8 * elements, bytes_accessed=14 * raw.size, transcendentals=elements),
        name="scan_ends",
    )(raw, conv, gate, gg, a2, b.reshape(-1), c.reshape(-1), cut.reshape(-1))


def scan_both(raw, conv, gate, gg, skip, a2, h0, q0, b, c, cut, seqs, fsplit=16, bsplit=16):
    blocks, states, groups, _ = a2.shape
    rows, inner = raw.shape
    tokens, _, _ = sizes(raw, seqs, states)
    width = groups * 128
    smem = pl.BlockSpec(memory_space=pltpu.SMEM)
    elements = raw.size * states
    token = token_spec(tokens, width)
    tiles = tokens // 8
    pair = pl.BlockSpec((None, tiles, groups, 128), lambda s, j: (j, s, 0, 0))
    pair_shape = jax.ShapeDtypeStruct((blocks, rows // 8, groups, 128), jnp.float32)
    low = jax.ShapeDtypeStruct((rows, inner), jnp.bfloat16)
    return pl.pallas_call(
        functools.partial(scan_kernel, groups, states, min(fsplit, states), min(bsplit, states)),
        grid=(seqs, blocks),
        in_specs=[token] * 4
        + [pl.BlockSpec((1, width), lambda s, j: (0, j)),
           pl.BlockSpec((None, states, groups, 128), lambda s, j: (j, 0, 0, 0)),
           state_spec(states, groups), state_spec(states, groups), smem, smem, smem],
        out_specs=[token] * 4 + [state_spec(states, groups), pair, pair,
                                 pl.BlockSpec((None, 8, width), lambda s, j: (s, 0, j))],
        out_shape=[low, low, low, jax.ShapeDtypeStruct((rows, inner), jnp.float32),
                   jax.ShapeDtypeStruct((seqs, blocks, states, groups, 128), jnp.float32),
                   pair_shape, pair_shape, jax.ShapeDtypeStruct((seqs, 8, inner), jnp.float32)],
        scratch_shapes=[pltpu.VMEM((tokens * groups, 128), jnp.float32)] * 5
        + [pltpu.VMEM((tokens, states, groups, 128), jnp.float32)],
        compiler_params=pltpu.CompilerParams(vmem_limit_bytes=VMEM_LIMIT),
        cost_estimate=pl.CostEstimate(flops=22 * elements, bytes_accessed=24 * raw.size, transcendentals=2 * elements),
        name="scan_both",
    )(raw, conv, gate, gg, skip.reshape(1, inner), a2, h0, q0, b.reshape(-1), c.reshape(-1), cut.reshape(-1))


def pair_sum(value, states):
    total = jnp.sum(value, axis=(0, 2))
    return total.reshape(-1, states)


from jax.sharding import PartitionSpec as P

EPSILON = 1e-05
BF16 = jnp.bfloat16


def from_behind(value, axis, by):
    devices = lax.axis_size(axis)
    pairs = [(i, i + by) for i in range(devices) if 0 <= i + by < devices]
    return lax.ppermute(value, axis, pairs)


def product(left, right, left_dim, right_dim):
    return lax.dot_general(
        left, right, (((left_dim,), (right_dim,)), ((), ())), preferred_element_type=jnp.float32
    )


def exchange_ends(last, total, back, axis):
    devices, here = lax.axis_size(axis), lax.axis_index(axis)
    everything = lax.all_gather(jnp.stack([last, total, back]), axis)
    state = jnp.zeros_like(last)
    for k in range(devices - 1):
        state = jnp.where(k < here, everything[k, 1] * state + everything[k, 0], state)
    adjoint = jnp.zeros_like(last)
    for k in reversed(range(1, devices)):
        adjoint = jnp.where(k > here, everything[k, 1] * adjoint + everything[k, 2], adjoint)
    return state, adjoint


def per_device(
    stream,
    norm_gain,
    in_weight,
    select_weight,
    delta_weight,
    delta_bias,
    out_weight,
    filter_weight,
    filter_bias,
    decay_log,
    skip_gain,
    segments,
    modality,
    valid,
    upstream,
):
    seqs, local_len, part_width = stream.shape
    width = norm_gain.shape[0]
    inner = out_weight.shape[0]
    states = decay_log.shape[0]
    reach = filter_weight.shape[0] - 1
    rows = seqs * local_len
    full_out = lax.all_gather(out_weight, "shard", axis=1, tiled=True)
    full_in = lax.all_gather(in_weight, "shard", axis=1, tiled=True)
    full_select = lax.all_gather(select_weight, "shard", axis=1, tiled=True)
    full_delta = lax.all_gather(delta_weight, "shard", axis=1, tiled=True)
    modes = full_in.shape[0]
    full_in = full_in.reshape(modes, width, 2 * inner)
    rank = full_delta.shape[1]
    mode_rows = modality.reshape(rows)
    masks = jnp.stack([(mode_rows == index).astype(BF16)[:, None] for index in range(modes)])
    masks_float = masks.astype(jnp.float32)
    valid_rows = valid.reshape(rows, 1).astype(jnp.float32)

    def apply_modes(values, weights, weight_dim):
        total = product(values * masks[0], weights[0], 1, weight_dim)
        for index in range(1, modes):
            total = total + product(values * masks[index], weights[index], 1, weight_dim)
        return total

    def modal_terms(values, grads):
        return jnp.stack([product(values * masks[index], grads, 0, 0) for index in range(modes)])

    g_mix = lax.all_gather(upstream, "tp", axis=2, tiled=True).reshape(rows, width) * valid_rows.astype(BF16)
    g_gated = product(g_mix, full_out, 1, 1)

    whole = lax.all_gather(stream, "tp", axis=2, tiled=True).reshape(rows, width).astype(jnp.float32)
    inverse = lax.rsqrt(jnp.mean(whole * whole, axis=1, keepdims=True) + EPSILON)
    normed = (whole * inverse * norm_gain).astype(BF16)
    projected = apply_modes(normed, full_in, 0)
    conv_in = projected[:, :inner].astype(BF16).reshape(seqs, local_len, inner)
    gate_in = projected[:, inner:]
    edge = from_behind(conv_in[:, local_len - reach :], "ctx", 1)
    extended = jnp.concatenate([edge, conv_in], axis=1).astype(jnp.float32)
    offset = lax.axis_index("ctx") * local_len
    padded = jnp.concatenate([jnp.full((seqs, reach), -1, jnp.int32), segments], axis=1)
    seg_ext = lax.dynamic_slice_in_dim(padded, offset, local_len + reach, 1)
    own_seg = seg_ext[:, reach:]
    same = [
        (seg_ext[:, reach - lag : reach - lag + local_len] == own_seg).astype(jnp.float32)[:, :, None]
        for lag in range(reach + 1)
    ]
    taps = [extended[:, reach - lag : reach - lag + local_len] for lag in range(reach + 1)]
    pre = jnp.zeros((seqs, local_len, inner), jnp.float32) + filter_bias
    for lag in range(reach + 1):
        pre = pre + filter_weight[reach - lag] * taps[lag] * same[lag]
    cut = (1.0 - same[1][:, :, 0]) * 1e30
    conv_out = jax.nn.silu(pre).astype(BF16).reshape(rows, inner)
    selected = lax.psum(apply_modes(conv_out, full_select, 1), "tp")
    delta_low = selected[:, :rank].astype(BF16)
    b_in = selected[:, rank : rank + states]
    c_out = selected[:, rank + states :]
    bias_rows = sum(masks_float[index] * delta_bias[index] for index in range(modes))
    raw = apply_modes(delta_low, full_delta, 0) + bias_rows

    neg_decay = -jnp.exp(decay_log)
    _, blocks, groups = sizes(raw, seqs, states)
    a2 = state_form(neg_decay * LOG2E, blocks, groups)
    ends = scan_ends(raw, conv_out, gate_in, g_gated, a2, b_in, c_out, cut, seqs)
    carried, behind = exchange_ends(*ends, "ctx")
    gated, g_gate, g_raw, g_conv, g_neg, g_b, g_c, g_skip = scan_both(
        raw, conv_out, gate_in, g_gated, skip_gain, a2, carried, behind, b_in, c_out, cut, seqs
    )

    out_terms = product(gated, g_mix, 0, 0).astype(BF16)
    out_grad = lax.psum_scatter(out_terms, ("shard", "ctx"), scatter_dimension=1, tiled=True)
    mix_local = (
        lax.psum_scatter(
            product(gated, full_out, 1, 0).astype(BF16), "tp", scatter_dimension=1, tiled=True
        ).astype(jnp.float32)
        * valid_rows
    )
    local_stream = stream.reshape(rows, part_width).astype(jnp.float32)
    output = (local_stream + mix_local).astype(BF16).reshape(seqs, local_len, part_width)
    stream_sq = jnp.sum(valid_rows * local_stream * local_stream)
    mixer_sq = jnp.sum(mix_local * mix_local)
    count = jnp.sum(valid_rows)
    skip_grad = jnp.sum(g_skip, axis=(0, 1))
    decay_grad = from_state_form(jnp.sum(g_neg, axis=0)) * neg_decay
    bias_grad = product(masks[:, :, 0], g_raw, 1, 0)
    delta_terms = modal_terms(delta_low, g_raw)
    g_low = apply_modes(g_raw, full_delta, 1)
    select_part = jnp.concatenate([g_low, pair_sum(g_b, states), pair_sum(g_c, states)], axis=1)
    g_sel_low = lax.psum(select_part, "tp").astype(BF16)
    select_terms = modal_terms(g_sel_low, conv_out)
    g_conv = g_conv + apply_modes(g_sel_low, full_select, 0)
    sig_pre = jax.nn.sigmoid(pre)
    g_pre = g_conv.reshape(seqs, local_len, inner) * sig_pre * (1.0 + pre * (1.0 - sig_pre))
    offset_grad = jnp.sum(g_pre, axis=(0, 1))
    filter_rows = [None] * (reach + 1)
    g_ext = jnp.zeros((seqs, local_len + reach, inner), jnp.float32)
    for lag in range(reach + 1):
        masked = g_pre * same[lag]
        filter_rows[reach - lag] = jnp.sum(masked * taps[lag], axis=(0, 1))
        g_ext = g_ext + jnp.pad(filter_weight[reach - lag] * masked, ((0, 0), (reach - lag, lag), (0, 0)))
    filter_grad = jnp.stack(filter_rows)
    returned = from_behind(g_ext[:, :reach], "ctx", -1)
    g_conv_in = g_ext[:, reach:] + jnp.pad(returned, ((0, 0), (local_len - reach, 0), (0, 0)))
    g_projected = jnp.concatenate([g_conv_in.reshape(rows, inner).astype(BF16), g_gate], axis=1)
    in_terms = modal_terms(normed, g_projected).astype(BF16).reshape(modes, width, 2, inner)
    in_grad = lax.psum_scatter(in_terms, ("shard", "ctx"), scatter_dimension=1, tiled=True)
    select_grad = lax.psum_scatter(select_terms, ("shard", "ctx"), scatter_dimension=1, tiled=True)
    delta_grad = lax.psum_scatter(delta_terms, ("shard", "ctx"), scatter_dimension=1, tiled=True)

    g_normed_part = apply_modes(g_projected, full_in, 1)
    row_part = jnp.sum(g_normed_part * norm_gain * whole, axis=1, keepdims=True)
    row_total = lax.psum(row_part, "tp")
    g_normed = lax.psum_scatter(
        g_normed_part.astype(BF16), "tp", scatter_dimension=1, tiled=True
    ).astype(jnp.float32)
    start = lax.axis_index("tp") * part_width
    own_gain = lax.dynamic_slice_in_dim(norm_gain, start, part_width, 0)
    g_stream = inverse * own_gain * g_normed - local_stream * inverse**3 * row_total / width
    gain_grad = jnp.sum(g_normed * local_stream * inverse, axis=0)
    upstream_local = upstream.reshape(rows, part_width).astype(jnp.float32)
    stream_gradient = (upstream_local + g_stream).astype(BF16).reshape(seqs, local_len, part_width)

    sums = lax.psum(
        (gain_grad, bias_grad, filter_grad, offset_grad, decay_grad, skip_grad, count), ("shard", "ctx")
    )
    squares = lax.psum((stream_sq, mixer_sq), ("shard", "ctx", "tp"))
    denominator = jnp.maximum(sums[6], 1.0) * width
    stream_rms = jnp.sqrt(squares[0] / denominator)
    mixer_rms = jnp.sqrt(squares[1] / denominator)
    return (
        output,
        stream_gradient,
        sums[0],
        in_grad.astype(jnp.float32),
        select_grad,
        delta_grad,
        sums[1],
        out_grad.astype(jnp.float32),
        sums[2],
        sums[3],
        sums[4],
        sums[5],
        stream_rms,
        mixer_rms,
    )


def solution(mesh):
    return jax.shard_map(
        per_device,
        mesh=mesh,
        in_specs=(
            P("shard", "ctx", "tp"),
            P(),
            P(None, "shard", None, "tp"),
            P(None, "shard", "tp"),
            P(None, "shard", "tp"),
            P(None, "tp"),
            P("tp", "shard"),
            P(None, "tp"),
            P("tp"),
            P(None, "tp"),
            P("tp"),
            P("shard", None),
            P("shard", "ctx"),
            P("shard", "ctx"),
            P("shard", "ctx", "tp"),
        ),
        out_specs=(
            P("shard", "ctx", "tp"),
            P("shard", "ctx", "tp"),
            P("tp"),
            P(None, ("shard", "ctx"), None, "tp"),
            P(None, ("shard", "ctx"), "tp"),
            P(None, ("shard", "ctx"), "tp"),
            P(None, "tp"),
            P("tp", ("shard", "ctx")),
            P(None, "tp"),
            P("tp"),
            P(None, "tp"),
            P("tp"),
            P(),
            P(),
        ),
        check_vma=False,
    )
```

profile of v0, /device:TPU:1, one launch (start us, length us, event | category | flops | bytes accessed | tf_op | source)
XLA Modules:
  0.0 1346.8 jit_solution(7996806601469471218)
XLA Ops:
  10.9 33.9 %all-gather.9.cloned.1.call-done = bf16[2,256,2048]{2,1,0:T(8,128)(2,1)} async-done(((bf16[2,256,1024]{2,1,0:T(8,128)(2,1)}), bf16[2,256,2048]{2,1,0:T(8,128)(2,1)}) %all-gather.9.cloned.1.call-update) | async-done | bytes 2097168 | tf_op jit(solution)/shard_map/all_gather | solution.py:357
  51.3 197.0 %all-gather.11.cloned.1.call-done = bf16[2,2048,2,2048]{3,2,1,0:T(2,128)(2,1)} async-done(((bf16[2,512,2,2048]{3,2,1,0:T(2,128)(2,1)}), bf16[2,2048,2,2048]{3,2,1,0:T(2,128)(2,1)}) %all-gather.11.cloned.1.call-update) | async-done | bytes 33554448 | tf_op jit(solution)/shard_map/all_gather | solution.py:334
  248.3 25.8 %fusion.68 = (bf16[1,2048,2,2048]{3,2,1,0:T(2,128)(2,1)S(1)}, bf16[1,2048,2,2048]{3,2,1,0:T(2,128)(2,1)}) fusion(bf16[2,2048,2,2048]{3,2,1,0:T(2,128)(2,1)} %all-gather.11.cloned.1.call-done), kind=kLoop, calls=%fused_computation.151 | loop fusion | bytes 67108864 | tf_op jit(solution)/shard_map/slice | solution.py:348
  274.2 17.6 %copy.82 = bf16[256,8,2,2048]{3,1,2,0:T(8,128)(2,1)} copy(bf16[256,8,2,2048]{3,2,1,0:T(2,128)(2,1)} %bitcast.199) | data formatting | bytes 33554432
  302.1 14.6 %fusion.78 = f32[512,4096]{1,0:T(8,128)} fusion(bf16[512,2048]{1,0:T(8,128)(2,1)S(1)} %bitcast.222, bf16[2048,4096]{1,0:T(8,128)(2,1)} %bitcast.205), kind=kOutput, calls=%fused_computation.161 | convolution fusion | flops 8589934592 | bytes 27262976 | tf_op jit(solution)/shard_map/dot_general | solution.py:293
  316.7 13.7 %convolution_add_fusion = f32[512,4096]{1,0:T(8,128)S(1)} fusion(f32[512,4096]{1,0:T(8,128)} %fusion.78, bf16[512,2048]{1,0:T(8,128)(2,1)S(1)} %bitcast.219, bf16[2048,4096]{1,0:T(8,128)(2,1)} %bitcast.207), kind=kOutput, calls=%fused_computation.4 | convolution fusion | flops 8592031744 | bytes 35651584 | tf_op jit(solution)/shard_map/dot_general | solution.py:293
  376.6 12.5 all-reduce.15.cloned.1.call-done
  391.6 16.2 %all-gather.15.cloned.1.call-done = bf16[2,128,2048]{2,1,0:T(8,128)(2,1)} async-done(((bf16[2,32,2048]{2,1,0:T(8,128)(2,1)}), bf16[2,128,2048]{2,1,0:T(8,128)(2,1)}) %all-gather.15.cloned.1.call-update) | async-done | bytes 1048592 | tf_op jit(solution)/shard_map/all_gather | solution.py:336
  413.0 33.8 %scan_ends.1 = (f32[2,2,16,8,128]{4,3,2,1,0:T(8,128)}, f32[2,2,16,8,128]{4,3,2,1,0:T(8,128)}, f32[2,2,16,8,128]{4,3,2,1,0:T(8,128)}) custom-call(f32[512,2048]{1,0:T(8,128)} %add_add_fusion.1.raw_ref, bf16[512,2048]{1,0:T(8,128)(2,1)} %bitcast.201, f32[512,2048]{1,0:T(8,128)} %slice.192.gate_ref, f32[512,2048]{1,0:T(8,128)} %fusion.79.gg_ref, ...), custom_call_target="tpu_custom_call" | custom-call | flops 134217728 | bytes 14680064 | tf_op jit(solution)/shard_map/scan_ends/pallas_call | solution.py:229
  448.9 63.2 %all-gather.21.cloned.1.call-done = f32[12,2,2,16,8,128]{5,4,3,2,1,0:T(8,128)} async-done(((f32[3,2,2,16,8,128]{5,4,3,2,1,0:T(8,128)}), f32[12,2,2,16,8,128]{5,4,3,2,1,0:T(8,128)}) %all-gather.21.cloned.1.call-update) | async-done | bytes 3145744 | tf_op jit(solution)/shard_map/all_gather | solution.py:300
  514.7 95.4 %scan_both.1 = (bf16[512,2048]{1,0:T(8,128)(2,1)}, bf16[512,2048]{1,0:T(8,128)(2,1)}, bf16[512,2048]{1,0:T(8,128)(2,1)}, f32[512,2048]{1,0:T(8,128)}, f32[2,2,16...) custom-call(f32[512,2048]{1,0:T(8,128)} %add_add_fusion.1.raw_ref, ...), custom_call_target="tpu_custom_call" | custom-call | flops 369098752 | bytes 25165824 | tf_op jit(solution)/shard_map/scan_both/pallas_call | solution.py:255
  618.0 11.2 all-reduce.18
  662.0 10.7 pad_add_fusion
  677.1 14.7 %fusion.2 = f32[512,2048]{1,0:T(8,128)} fusion(bf16[2048,4096]{1,0:T(8,128)(2,1)} %bitcast.208, bf16[512]{0:T(512)(128)(2,1)S(1)} %bitcast.258, bf16[512,2048]{1,0:T(8,128)(2,1)} %get-tuple-element.33, bf16[512,2048]{1,0:T(8,128)(2,1)S(1)} %bitcast.211), kind=kOutput, calls=%fused_computation.16 | convolution fusion | flops 8602517504 | bytes 25166848 | tf_op jit(solution)/shard_map/dot_general | solution.py:293
  691.8 15.7 %fusion.1 = (f32[512]{0:T(512)S(1)}, bf16[512,2048]{1,0:T(8,128)(2,1)}) fusion(f32[2048]{0:T(1024)S(1)} %copy-done.38, bf16[2,256,2048]{2,1,0:T(8,128)(2,1)S(1)} %copy-done.10, f32[512,2048]{1,0:T(8,128)} %fusion.2, bf16[2048,4096]{1,0:T(8,128)(2,1)} %bitcast.206, bf16[512]{0:T(512)(128)(2,1)S(1)} %bitcast.252, bf16[512,2048]{1,0:T(8,128)(2,1)} %get-tuple-element.33, ...), kind=kOutput, calls=%fused_computation.11 | convolution fusion | flops 8608808960 | bytes 29371392 | tf_op jit(solution)/shard_map/dot_general | solution.py:293
  717.6 12.3 copy.79
  742.2 15.1 %convert_bitcast_fusion.1 = bf16[1,2048,2,2048]{3,1,2,0:T(8,128)(2,1)} fusion(bf16[512,2048,1]{1,0,2:T(8,128)(2,1)} %bitcast.221, bf16[2,2048,512]{2,1,0:T(8,128)(2,1)} %bitcast.215), kind=kOutput, calls=%fused_computation.2 | convolution fusion | flops 8598323200 | bytes 23068672 | tf_op jit(solution)/shard_map/dot_general | solution.py:293
  757.3 12.6 convert_bitcast_fusion
  769.9 22.9 %pad_maximum_fusion = bf16[2,2048,2,2048]{3,1,2,0:T(8,128)(2,1)} fusion(bf16[1,2048,2,2048]{3,1,2,0:T(8,128)(2,1)} %convert_bitcast_fusion, bf16[1,2048,2,2048]{3,1,2,0:T(8,128)(2,1)} %convert_bitcast_fusion.1), kind=kLoop, calls=%fused_computation | loop fusion | flops 16777216 | bytes 67108864 | tf_op jit(solution)/shard_map/stack | solution.py:352
  806.7 17.0 %reduce-scatter.10.cloned.1.call-done = bf16[512,1024]{1,0:T(8,128)(2,1)} async-done(((bf16[512,2048]{1,0:T(8,128)(2,1)}), bf16[512,1024]{1,0:T(8,128)(2,1)}) %reduce-scatter.10.cloned.1.call-update) | async-done | bytes 1048592 | tf_op jit(solution)/shard_map/reduce_scatter | solution.py:438
  828.3 39.9 %all-reduce.7 = (f32[]{:T(128)}, f32[]{:T(128)}) all-reduce(f32[]{:T(128)} %fusion.14, f32[]{:T(128)} %get-tuple-element.131), channel_id=1, replica_groups=mesh['shard'=4,'ctx'=4,'tp'=2] {'shard','ctx','tp'}, use_global_device_ids=true, to_apply=%region_28.29 | all-reduce | flops 2 | bytes 16 | tf_op jit(solution)/shard_map/psum | solution.py:451
  868.2 64.5 %all-reduce.19 = (f32[1024]{0:T(1024)}, f32[2,2048]{1,0:T(2,128)}, f32[4,2048]{1,0:T(4,128)}, f32[2048]{0:T(1024)}, f32[2048]{0:T(1024)}, /*index=5*/f32[]{:T(128)}) all-reduce(f32[1024]{0:T(1024)S(1)} %get-tuple-element.134, f32[2,2048]{1,0:T(2,128)S(1)} %fusion.63, ...), channel_id=1, replica_groups=mesh['shard'=4,'ctx'=4,'tp'=2] {'shard','ctx'}, use_global_device_ids=true, to_apply=%region_10.11 | all-reduce | flops 17409 | bytes 139272 | tf_op jit(solution)/shard_map/psum | solution.py:448
  938.4 334.8 %reduce-scatter.12.cloned.1.call-done = bf16[2,128,2,2048]{3,1,2,0:T(8,128)(2,1)} async-done(((bf16[2,2048,2,2048]{3,1,2,0:T(8,128)(2,1)}), bf16[2,128,2,2048]{3,1,2,0:T(8,128)(2,1)}) %reduce-scatter.12.cloned.1.call-update) | async-done | bytes 2097168 | tf_op jit(solution)/shard_map/reduce_scatter | solution.py:431
  1278.9 57.9 %reduce-scatter.14.cloned.1.call-done = f32[2,8,2048]{2,1,0:T(8,128)} async-done(((f32[2,128,2048]{2,1,0:T(8,128)}), f32[2,8,2048]{2,1,0:T(8,128)}) %reduce-scatter.14.cloned.1.call-update) | async-done | bytes 131088 | tf_op jit(solution)/shard_map/reduce_scatter | solution.py:433
  (235 shorter events, 173.8 us)
Async XLA Ops:
  7.2 37.6 %all-gather.9.cloned.1.call-start = ((), (), s32[]{:S(2)}) async-start(), calls=%async_computation.5 | async-start | bytes 3145728 | tf_op jit(solution)/shard_map/all_gather | solution.py:357
  7.9 240.4 %all-gather.11.cloned.1.call-start = ((), (), s32[]{:S(2)}) async-start(), calls=%async_computation.6 | async-start | bytes 41943040 | tf_op jit(solution)/shard_map/all_gather | solution.py:334
  8.7 38.8 %copy-start.37 = (f32[2048]{0:T(1024)S(1)}, f32[2048]{0:T(1024)}, u32[]{:S(2)}) copy-start(f32[2048]{0:T(1024)} %param.16) | copy-start | bytes 24580
  8.7 334.6 %all-gather.13.cloned.1.call-start = ((), (), s32[]{:S(2)}) async-start(), calls=%async_computation.7 | async-start | bytes 1638400 | tf_op jit(solution)/shard_map/all_gather | solution.py:335
  9.4 343.2 %all-gather.17.cloned.1.call-start = ((), (), s32[]{:S(2)}) async-start(), calls=%async_computation.10 | async-start | bytes 3145728 | tf_op jit(solution)/shard_map/all_gather | solution.py:354
  10.0 352.4 %all-gather.19.cloned.1.call-start = ((), (), s32[]{:S(2)}) async-start(), calls=%async_computation.11 | async-start | bytes 10485760 | tf_op jit(solution)/shard_map/all_gather | solution.py:333
  10.6 378.4 %all-reduce.15.cloned.1.call-start = ((), (), s32[]{:S(2)}) async-start(), calls=%async_computation.8 | async-start | bytes 655360 | tf_op jit(solution)/shard_map/psum | solution.py:379
  51.3 265.4 %copy-start.20 = (bf16[2,256,2048]{2,1,0:T(8,128)(2,1)}, bf16[2,256,2048]{2,1,0:T(8,128)(2,1)S(1)}, u32[]{:S(2)}) copy-start(bf16[2,256,2048]{2,1,0:T(8,128)(2,1)S(1)} %get-tuple-element.127) | copy-start | bytes 6291460
  330.8 4.5 collective-permute-start
  349.3 58.5 %all-gather.15.cloned.1.call-start = ((), (), s32[]{:S(2)}) async-start(), calls=%async_computation.9 | async-start | bytes 1310720 | tf_op jit(solution)/shard_map/all_gather | solution.py:336
  350.1 161.9 %all-gather.21.cloned.1.call-start = ((), (), s32[]{:S(2)}) async-start(), calls=%async_computation.16 | async-start | bytes 3932160 | tf_op jit(solution)/shard_map/all_gather | solution.py:300
  351.9 20.0 %copy-start.35 = (f32[1,2,2,128]{3,1,2,0:T(2,128)}, f32[1,2,2,128]{3,1,2,0:T(2,128)S(1)}, u32[]{:S(2)}) copy-start(f32[1,2,2,128]{3,1,2,0:T(2,128)S(1)} %copy.86) | copy-start | bytes 6148
  354.4 17.5 %copy-start.19 = (bf16[512,2048]{1,0:T(8,128)(2,1)}, bf16[512,2048]{1,0:T(8,128)(2,1)S(1)}, u32[]{:S(2)}) copy-start(bf16[512,2048]{1,0:T(8,128)(2,1)S(1)} %bitcast_multiply_fusion.1) | copy-start | bytes 6291460
  389.0 20.8 %copy-start.16 = (f32[512,160]{0,1:T(8,128)S(1)}, f32[512,160]{0,1:T(8,128)}, u32[]{:S(2)}) copy-start(f32[512,160]{0,1:T(8,128)} %all-reduce.15.cloned.1.call-done) | copy-start | bytes 983044
  448.8 356.2 %all-reduce.17.cloned.1.call-start = ((), (), s32[]{:S(2)}) async-start(), calls=%async_computation.18 | async-start | bytes 5505024
  647.0 25.9 %collective-permute-start.1 = (f32[2,3,2048]{2,1,0:T(4,128)S(1)}, f32[2,3,2048]{2,1,0:T(4,128)S(1)}, u32[]{:S(2)}, u32[]{:S(2)}) collective-permute-start(f32[2,3,2048]{2,1,0:T(4,128)S(1)} %pad_add_fusion.1), channel_id=1, source_target_pairs={{2,0},{4,2},{6,4},{3,1},{5,3},{7,5},{10,8},{12,10},{14,12},{11,9},... | collective-permute-start | bytes 147464 | tf_op jit(solution)/shard_map/ppermute | solution.py:289
  652.8 153.8 %reduce-scatter.8.cloned.1.call-start = ((), (), s32[]{:S(2)}) async-start(), calls=%async_computation.12 | async-start | bytes 3145728 | tf_op jit(solution)/shard_map/reduce_scatter | solution.py:398
  672.7 151.0 %reduce-scatter.10.cloned.1.call-start = ((), (), s32[]{:S(2)}) async-start(), calls=%async_computation.13 | async-start | bytes 3145728 | tf_op jit(solution)/shard_map/reduce_scatter | solution.py:438
  707.5 228.5 %reduce-scatter.16.cloned.1.call-start = ((), (), s32[]{:S(2)}) async-start(), calls=%async_computation.17 | async-start | bytes 8912896
  730.0 543.2 %reduce-scatter.12.cloned.1.call-start = ((), (), s32[]{:S(2)}) async-start(), calls=%async_computation.14 | async-start | bytes 35651584 | tf_op jit(solution)/shard_map/reduce_scatter | solution.py:431
  792.8 544.1 %reduce-scatter.14.cloned.1.call-start = ((), (), s32[]{:S(2)}) async-start(), calls=%async_computation.15 | async-start | bytes 2228224 | tf_op jit(solution)/shard_map/reduce_scatter | solution.py:433
  795.4 28.3 %copy-start.36 = (f32[1,2,2,128]{3,1,2,0:T(2,128)S(1)}, f32[1,2,2,128]{3,1,2,0:T(2,128)}, u32[]{:S(2)}) copy-start(f32[1,2,2,128]{3,1,2,0:T(2,128)} %copy-done.35) | copy-start | bytes 6148
  800.4 67.7 %copy-start.30 = (f32[2048]{0:T(1024)S(1)}, f32[2048]{0:T(1024)}, u32[]{:S(2)}) copy-start(f32[2048]{0:T(1024)} %get-tuple-element.96) | copy-start | bytes 24580
  937.3 399.6 %copy-start.26 = (f32[16,2048]{1,0:T(8,128)S(1)}, f32[16,2048]{1,0:T(8,128)}, u32[]{:S(2)}) copy-start(f32[16,2048]{1,0:T(8,128)} %get-tuple-element.164) | copy-start | bytes 393220
  (46 other events, 241.4 us)
Sparse Core Ops, SparseCore 0:
  9.6 35.1 all-gather.8
  46.4 201.9 all-gather.10
  249.9 18.1 all-gather.12
  269.5 32.7 all-gather.16
  303.7 58.7 all-gather.18
  365.1 23.8 all-reduce.14
  390.6 17.1 all-gather.14
  448.9 63.0 all-gather.20
  653.0 101.5 all-reduce.16
  756.8 32.6 reduce-scatter.7
  791.7 31.9 reduce-scatter.9
  828.1 107.8 reduce-scatter.15
  940.8 332.2 reduce-scatter.11
  1277.8 59.0 reduce-scatter.13
where the time goes:
time: 1360 us; the launch traced here: 1350 us
  waiting for transfers between devices  747 us (55%)
  matrix products  135 us (10%)
  Pallas kernels  129 us (9%)
  blocking collectives  120 us (9%)
  local copies, waits for them, and re-layouts  109 us (8%)
  other arithmetic  80.9 us (6%)
  between operations  20.1 us (1%)
    reduce_scatter x1, waiting for transfers between devices, per_device(): lax.psum_scatter(in_terms, ('shard', 'ctx'), scatter_dimension=1, tiled=T...  335 us
    all_gather x1, waiting for transfers between devices, per_device(): full_in = lax.all_gather(in_weight, 'shard', axis=1, tiled=True)  197 us
    dot_general x22, matrix products, product(): lax.dot_general(left, right, (((left_dim,), (right_dim,)), ((), ())), pre...  135 us
    pallas_call x1, Pallas kernels, scan_both(): pl.pallas_call(functools.partial(scan_kernel, groups, states, min(fsplit,...  95.4 us
    psum x1, blocking collectives, per_device(): lax.psum((gain_grad, bias_grad, filter_grad, offset_grad, decay_grad, ski...  64.5 us
    unnamed x122, local copies, waits for them, and re-layouts  64.3 us
    all_gather x1, waiting for transfers between devices, exchange_ends(): everything = lax.all_gather(jnp.stack([last, total, back]), axis)  63.2 us
    reduce_scatter x1, waiting for transfers between devices, per_device(): lax.psum_scatter(delta_terms, ('shard', 'ctx'), scatter_dimension=1, tile...  57.9 us
  transfers between devices with their start and end apart: 16, of which 11 were waited for; matrix products, arithmetic and copies ran while one was open for 21% of the time, Pallas kernels for 0%

commit v1 on v0

--- a/solution.py
+++ b/solution.py
@@ -211,70 +211,420 @@
     return value.transpose(1, 0, 2, 3).reshape(states, blocks * groups * lanes)
 
 
-def token_spec(tokens, width):
-    return pl.BlockSpec((tokens, width), lambda s, j: (s, j))
+def token_spec(tokens, width, block):
+    return pl.BlockSpec((tokens, width), lambda s: (s, block))
 
 
 def state_spec(states, groups):
-    return pl.BlockSpec((None, None, states, groups, 128), lambda s, j: (s, j, 0, 0, 0))
-
-
-def scan_ends(raw, conv, gate, gg, a2, b, c, cut, seqs, split=16):
-    blocks, states, groups, _ = a2.shape
-    tokens, _, _ = sizes(raw, seqs, states)
+    return pl.BlockSpec((None, states, groups, 128), lambda s: (s, 0, 0, 0))
+
+
+def scan_ends(raw, conv, gate, gg, a2, b, c, cut, seqs, block):
+    states, groups, _ = a2.shape
+    tokens = raw.shape[0] // seqs
     width = groups * 128
     smem = pl.BlockSpec(memory_space=pltpu.SMEM)
-    out = jax.ShapeDtypeStruct((seqs, blocks, states, groups, 128), jnp.float32)
-    elements = raw.size * states
+    out = jax.ShapeDtypeStruct((seqs, states, groups, 128), jnp.float32)
+    elements = raw.shape[0] * width * states
     return pl.pallas_call(
-        functools.partial(ends_kernel, groups, states, min(split, states)),
-        grid=(seqs, blocks),
-        in_specs=[token_spec(tokens, width)] * 4
-        + [pl.BlockSpec((None, states, groups, 128), lambda s, j: (j, 0, 0, 0)), smem, smem, smem],
+        functools.partial(ends_kernel, groups, states, states),
+        grid=(seqs,),
+        in_specs=[token_spec(tokens, width, block)] * 4
+        + [pl.BlockSpec((states, groups, 128), lambda s: (0, 0, 0)), smem, smem, smem],
         out_specs=[state_spec(states, groups)] * 3,
         out_shape=[out] * 3,
         scratch_shapes=[pltpu.VMEM((tokens * groups, 128), jnp.float32)] * 3,
         compiler_params=pltpu.CompilerParams(vmem_limit_bytes=VMEM_LIMIT),
-        cost_estimate=pl.CostEstimate(flops=8 * elements, bytes_accessed=14 * raw.size, transcendentals=elements),
+        cost_estimate=pl.CostEstimate(flops=8 * elements, bytes_accessed=elements, transcendentals=elements),
         name="scan_ends",
     )(raw, conv, gate, gg, a2, b.reshape(-1), c.reshape(-1), cut.reshape(-1))
 
 
-def scan_both(raw, conv, gate, gg, skip, a2, h0, q0, b, c, cut, seqs, fsplit=16, bsplit=16):
-    blocks, states, groups, _ = a2.shape
+def scan_both(raw, conv, gate, gg, skip, a2, h0, q0, b, c, cut, seqs, block):
+    states, groups, _ = a2.shape
     rows, inner = raw.shape
-    tokens, _, _ = sizes(raw, seqs, states)
+    tokens = rows // seqs
     width = groups * 128
     smem = pl.BlockSpec(memory_space=pltpu.SMEM)
-    elements = raw.size * states
-    token = token_spec(tokens, width)
+    elements = rows * width * states
+    token = token_spec(tokens, width, block)
     tiles = tokens // 8
-    pair = pl.BlockSpec((None, tiles, groups, 128), lambda s, j: (j, s, 0, 0))
-    pair_shape = jax.ShapeDtypeStruct((blocks, rows // 8, groups, 128), jnp.float32)
-    low = jax.ShapeDtypeStruct((rows, inner), jnp.bfloat16)
+    own = pl.BlockSpec((tokens, width), lambda s: (s, 0))
+    pair = pl.BlockSpec((tiles, groups, 128), lambda s: (s, 0, 0))
+    pair_shape = jax.ShapeDtypeStruct((rows // 8, groups, 128), jnp.float32)
+    low = jax.ShapeDtypeStruct((rows, width), jnp.bfloat16)
     return pl.pallas_call(
-        functools.partial(scan_kernel, groups, states, min(fsplit, states), min(bsplit, states)),
-        grid=(seqs, blocks),
+        functools.partial(scan_kernel, groups, states, states, states),
+        grid=(seqs,),
         in_specs=[token] * 4
-        + [pl.BlockSpec((1, width), lambda s, j: (0, j)),
-           pl.BlockSpec((None, states, groups, 128), lambda s, j: (j, 0, 0, 0)),
+        + [pl.BlockSpec((1, width), lambda s: (0, block)),
+           pl.BlockSpec((states, groups, 128), lambda s: (0, 0, 0)),
            state_spec(states, groups), state_spec(states, groups), smem, smem, smem],
-        out_specs=[token] * 4 + [state_spec(states, groups), pair, pair,
-                                 pl.BlockSpec((None, 8, width), lambda s, j: (s, 0, j))],
-        out_shape=[low, low, low, jax.ShapeDtypeStruct((rows, inner), jnp.float32),
-                   jax.ShapeDtypeStruct((seqs, blocks, states, groups, 128), jnp.float32),
-                   pair_shape, pair_shape, jax.ShapeDtypeStruct((seqs, 8, inner), jnp.float32)],
+        out_specs=[own] * 4 + [state_spec(states, groups), pair, pair,
+                               pl.BlockSpec((None, 8, width), lambda s: (s, 0, 0))],
+        out_shape=[low, low, low, jax.ShapeDtypeStruct((rows, width), jnp.float32),
+                   jax.ShapeDtypeStruct((seqs, states, groups, 128), jnp.float32),
+                   pair_shape, pair_shape, jax.ShapeDtypeStruct((seqs, 8, width), jnp.float32)],
         scratch_shapes=[pltpu.VMEM((tokens * groups, 128), jnp.float32)] * 5
         + [pltpu.VMEM((tokens, states, groups, 128), jnp.float32)],
         compiler_params=pltpu.CompilerParams(vmem_limit_bytes=VMEM_LIMIT),
-        cost_estimate=pl.CostEstimate(flops=22 * elements, bytes_accessed=24 * raw.size, transcendentals=2 * elements),
+        cost_estimate=pl.CostEstimate(flops=22 * elements, bytes_accessed=2 * elements, transcendentals=2 * elements),
         name="scan_both",
     )(raw, conv, gate, gg, skip.reshape(1, inner), a2, h0, q0, b.reshape(-1), c.reshape(-1), cut.reshape(-1))
 
 
 def pair_sum(value, states):
-    total = jnp.sum(value, axis=(0, 2))
-    return total.reshape(-1, states)
+    return jnp.sum(value, axis=1).reshape(-1, states)
+
+
+MESH = pl.DeviceIdType.MESH
+
+
+def gather_kernel(chunks, conv_ref, gate_ref, out_ref, conv_full, gate_full, out_full, local_sem, core_send,
+                  core_recv, y_send, y_recv, z_send, z_recv, pass_send, pass_recv, rest_send, rest_recv):
+    shard, ctx = lax.axis_index("shard"), lax.axis_index("ctx")
+    mine, far = shard, lax.rem(shard + 2, 4)
+    core = {"shard": shard + 1 - 2 * lax.rem(shard, 2)}
+    across = {"shard": far}
+    side = {"ctx": ctx + 1 - 2 * lax.rem(ctx, 2)}
+    half = lax.rem(ctx, 2)
+    depth = conv_ref.shape[1]
+    columns = out_ref.shape[1]
+    piece = depth // 2 // chunks
+    piece_out = out_ref.shape[0] // 2 // chunks
+
+    barrier = pltpu.get_barrier_semaphore()
+    for peer in (core, across, side):
+        pl.semaphore_signal(barrier, inc=1, device_id=peer, device_id_type=MESH)
+    pl.semaphore_wait(barrier, 3)
+
+    def views(owner, part, i):
+        rows = pl.ds(pl.multiple_of(owner * depth + (part * chunks + i) * piece, piece), piece)
+        tall = pl.ds(pl.multiple_of((part * chunks + i) * piece_out, piece_out), piece_out)
+        wide = pl.ds(pl.multiple_of(owner * columns, columns), columns)
+        return conv_full.at[:, rows], gate_full.at[:, rows], out_full.at[tall, wide]
+
+    def own(part, i):
+        rows = pl.ds(pl.multiple_of((part * chunks + i) * piece, piece), piece)
+        tall = pl.ds(pl.multiple_of((part * chunks + i) * piece_out, piece_out), piece_out)
+        return conv_ref.at[:, rows], gate_ref.at[:, rows], out_ref.at[tall, :]
+
+    def send(source, target, to, send_sem, recv_sem):
+        copies = [
+            pltpu.make_async_remote_copy(src_ref=s, dst_ref=t, send_sem=send_sem.at[k], recv_sem=recv_sem.at[k],
+                                         device_id=to, device_id_type=MESH)
+            for k, (s, t) in enumerate(zip(source, target))
+        ]
+        for copy in copies:
+            copy.start()
+        return copies
+
+    def cross(i):
+        return send(own(half, i), views(mine, half, i), across, y_send.at[i], y_recv.at[i])
+
+    to_far = [cross(i) for i in range(min(2, chunks))]
+    rows = pl.ds(pl.multiple_of(mine * depth, depth), depth)
+    wide = pl.ds(pl.multiple_of(mine * columns, columns), columns)
+    source = (conv_ref, gate_ref, out_ref)
+    place = (conv_full.at[:, rows], gate_full.at[:, rows], out_full.at[:, wide])
+    stay = [pltpu.make_async_copy(s, t, local_sem.at[k]) for k, (s, t) in enumerate(zip(source, place))]
+    for copy in stay:
+        copy.start()
+    to_core = send(source, place, core, core_send, core_recv)
+    onward = []
+    for i in range(chunks):
+        for copy in to_far[i]:
+            copy.wait()
+        if i + 2 < chunks:
+            to_far.append(cross(i + 2))
+        held = views(far, half, i)
+        onward.append(send(held, held, side, z_send.at[i], z_recv.at[i]))
+        to_core += send(held, held, core, pass_send.at[i], pass_recv.at[i])
+    for i in range(chunks):
+        for copy in onward[i]:
+            copy.wait_recv()
+        held = views(far, 1 - half, i)
+        to_core += send(held, held, core, rest_send.at[i], rest_recv.at[i])
+    for copy in stay:
+        copy.wait()
+    for copy in to_core:
+        copy.wait()
+    for i in range(chunks):
+        for copy in onward[i]:
+            copy.wait_send()
+
+
+def gather_weights(in_own, out_own, chunks=8):
+    _, modes, depth, inner = in_own.shape
+    any_space = pl.BlockSpec(memory_space=pl.ANY)
+    vmem = pl.BlockSpec(memory_space=pltpu.VMEM)
+    many = pltpu.SemaphoreType.DMA((chunks, 3))
+    three = pltpu.SemaphoreType.DMA((3,))
+    full = jax.ShapeDtypeStruct((modes, 4 * depth, inner), in_own.dtype)
+    return pl.pallas_call(
+        functools.partial(gather_kernel, chunks),
+        in_specs=[vmem] * 3,
+        out_specs=[any_space] * 3,
+        out_shape=[full, full, jax.ShapeDtypeStruct((inner, 4 * out_own.shape[1]), out_own.dtype)],
+        scratch_shapes=[three] * 3 + [many] * 8,
+        compiler_params=pltpu.CompilerParams(collective_id=1, has_side_effects=True, vmem_limit_bytes=32 * 2**20),
+        cost_estimate=pl.CostEstimate(flops=0, bytes_accessed=400_000_000, transcendentals=0),
+        name="gather_weights",
+    )(in_own[0], in_own[1], out_own)
+
+
+def finish_kernel(x_ref, gate_ref, conv_ref, gated_ref, sum_ref, blocks, part, below, above, y_send, y_recv,
+                  core_send, core_recv, pass_send, pass_recv, local_sem, up_send, up_recv, down_send, down_recv):
+    shard, ctx = lax.axis_index("shard"), lax.axis_index("ctx")
+    far = lax.rem(shard + 2, 4)
+    core = {"shard": shard + 1 - 2 * lax.rem(shard, 2)}
+    across = {"shard": far}
+    jobs, units, last = blocks.shape[0], part.shape[0], 3
+    tokens, width = gate_ref.shape
+    deep = sum_ref.shape[1]
+    up, down = {"ctx": ctx + 1}, {"ctx": ctx - 1}
+
+    barrier = pltpu.get_barrier_semaphore()
+    for peer in (core, across):
+        pl.semaphore_signal(barrier, inc=1, device_id=peer, device_id_type=MESH)
+
+    @pl.when(ctx < last)
+    def _():
+        pl.semaphore_signal(barrier, inc=1, device_id=up, device_id_type=MESH)
+
+    @pl.when(ctx > 0)
+    def _():
+        pl.semaphore_signal(barrier, inc=1, device_id=down, device_id_type=MESH)
+
+    pl.semaphore_wait(barrier, 2 + jnp.where(ctx < last, 1, 0) + jnp.where(ctx > 0, 1, 0))
+
+    sources = [gate_ref, conv_ref.at[:, pl.ds(0, width)], conv_ref.at[:, pl.ds(width, width)], gated_ref]
+
+    def rows_of(owner):
+        return pl.ds(pl.multiple_of(owner * tokens, tokens), tokens)
+
+    def remote(source, target, send_sem, recv_sem, to):
+        return pltpu.make_async_remote_copy(src_ref=source, dst_ref=target, send_sem=send_sem, recv_sem=recv_sem,
+                                            device_id=to, device_id_type=MESH)
+
+    def cross(j):
+        return remote(sources[j], blocks.at[j, rows_of(shard)], y_send.at[j], y_recv.at[j], across)
+
+    def pair(j):
+        return remote(sources[j], blocks.at[j, rows_of(shard)], core_send.at[j], core_recv.at[j], core)
+
+    def onward(j):
+        held = blocks.at[j, rows_of(far)]
+        return remote(held, held, pass_send.at[j], pass_recv.at[j], core)
+
+    def stay(j):
+        return pltpu.make_async_copy(sources[j], blocks.at[j, rows_of(shard)], local_sem.at[j])
+
+    def advance(j):
+        cross(j).wait()
+        onward(j).start()
+        if j + 2 < jobs:
+            cross(j + 2).start()
+
+    def hop(u, k, buffer, send_sem, recv_sem, to):
+        rows = pl.ds(pl.multiple_of(k * deep, deep), deep)
+        return remote(part.at[u, rows], buffer.at[u, rows], send_sem.at[u, k], recv_sem.at[u, k], to)
+
+    def going_up(u, k):
+        return hop(u, k, below, up_send, up_recv, up)
+
+    def going_down(u, k):
+        return hop(u, k, above, down_send, down_recv, down)
+
+    def add(u, k, buffer):
+        rows = pl.ds(k * deep, deep)
+        total = part[u, rows, :].astype(jnp.float32) + buffer[u, rows, :].astype(jnp.float32)
+        part[u, rows, :] = total.astype(part.dtype)
+
+    for j in range(min(2, jobs)):
+        cross(j).start()
+    for j in range(jobs):
+        stay(j).start()
+        pair(j).start()
+    advance(0)
+
+    def step(t, _):
+        for j in range(jobs):
+            @pl.when(t == 2 * j)
+            def _():
+                stay(j).wait()
+                pair(j).wait()
+                onward(j).wait()
+
+        @pl.when(t < units)
+        def _():
+            job = t // 2
+            which = jnp.where(t == 2 * (jobs - 1), 2, lax.rem(t, 2))
+            for c in range(width // 256):
+                lanes = slice(c * 256, c * 256 + 256)
+                part[t, :, lanes] = jnp.dot(
+                    x_ref[which], blocks[job, :, lanes], preferred_element_type=jnp.float32
+                ).astype(part.dtype)
+
+        u = t - ctx
+
+        @pl.when((u >= 0) & (u < units))
+        def _():
+            for k in range(last, 0, -1):
+                @pl.when(k > ctx)
+                def _():
+                    @pl.when(ctx > 0)
+                    def _():
+                        going_up(u, k).wait_recv()
+                        add(u, k, below)
+
+                    going_up(u, k).start()
+
+        v = t - (last - ctx)
+
+        @pl.when((v >= 0) & (v < units))
+        def _():
+            for k in range(last):
+                @pl.when(k < ctx)
+                def _():
+                    @pl.when(ctx < last)
+                    def _():
+                        going_down(v, k).wait_recv()
+                        add(v, k, above)
+
+                    going_down(v, k).start()
+
+        w = t - last
+
+        @pl.when(w >= 0)
+        def _():
+            rows = pl.ds(pl.multiple_of(ctx * deep, deep), deep)
+            sum_ref[w] = part[w, rows, :].astype(jnp.float32)
+
+            @pl.when(ctx > 0)
+            def _():
+                going_up(w, ctx).wait_recv()
+                sum_ref[w] += below[w, rows, :].astype(jnp.float32)
+
+            @pl.when(ctx < last)
+            def _():
+                going_down(w, ctx).wait_recv()
+                sum_ref[w] += above[w, rows, :].astype(jnp.float32)
+
+        for j in range(1, jobs):
+            @pl.when(t == 2 * j - 1)
+            def _():
+                advance(j)
+
+        return 0
+
+    lax.fori_loop(0, units + last, step, 0)
+
+    def drain(u, _):
+        for k in range(last + 1):
+            @pl.when(k > ctx)
+            def _():
+                going_up(u, k).wait_send()
+
+            @pl.when(k < ctx)
+            def _():
+                going_down(u, k).wait_send()
+
+        return 0
+
+    lax.fori_loop(0, units, drain, 0)
+
+
+def finish_weights(x, g_gate, g_conv_in, gated):
+    _, features, group = x.shape
+    tokens, width = g_gate.shape
+    jobs, units = 4, 7
+    deep = features // 4
+    any_space = pl.BlockSpec(memory_space=pl.ANY)
+    vmem = pl.BlockSpec(memory_space=pltpu.VMEM)
+    sums = pltpu.SemaphoreType.DMA((units, 4))
+    job_sems = pltpu.SemaphoreType.DMA((jobs,))
+    flops = 2 * units * features * group * width
+    return pl.pallas_call(
+        finish_kernel,
+        in_specs=[vmem, any_space, any_space, any_space],
+        out_specs=vmem,
+        out_shape=jax.ShapeDtypeStruct((units, deep, width), jnp.float32),
+        scratch_shapes=[pltpu.VMEM((jobs, group, width), jnp.bfloat16)]
+        + [pltpu.VMEM((units, features, width), jnp.bfloat16)] * 3
+        + [job_sems] * 7 + [sums] * 4,
+        compiler_params=pltpu.CompilerParams(collective_id=2, has_side_effects=True, vmem_limit_bytes=VMEM_LIMIT),
+        cost_estimate=pl.CostEstimate(flops=flops, bytes_accessed=500_000_000, transcendentals=0),
+        name="finish_weights",
+    )(x, g_gate, g_conv_in, gated)
+
+
+def small_kernel(in_ref, out_ref, x_in, mine, y_in, z_in, x_sem, a_send, a_recv, b_send, b_recv, c_send, c_recv):
+    shard, ctx, tp = lax.axis_index("shard"), lax.axis_index("ctx"), lax.axis_index("tp")
+    quarter = out_ref.shape[0] // 4
+    other = {"tp": 1 - tp}
+
+    def shard_peer(k):
+        return {"shard": lax.rem(shard + k, 4)}
+
+    def ctx_peer(k):
+        return {"ctx": lax.rem(ctx + k, 4)}
+
+    barrier = pltpu.get_barrier_semaphore()
+    pl.semaphore_signal(barrier, inc=1, device_id=other, device_id_type=MESH)
+    for k in range(1, 4):
+        pl.semaphore_signal(barrier, inc=1, device_id=shard_peer(k), device_id_type=MESH)
+        pl.semaphore_signal(barrier, inc=1, device_id=ctx_peer(k), device_id_type=MESH)
+    pl.semaphore_wait(barrier, 7)
+
+    def remote(source, target, send_sem, recv_sem, to):
+        copy = pltpu.make_async_remote_copy(src_ref=source, dst_ref=target, send_sem=send_sem, recv_sem=recv_sem,
+                                            device_id=to, device_id_type=MESH)
+        copy.start()
+        return copy
+
+    def rows_of(k):
+        return pl.ds(pl.multiple_of(k * quarter, 8), quarter)
+
+    total = in_ref.shape[0]
+    copy = remote(in_ref.at[pl.ds(total - 8, 8)], x_in, x_sem.at[0], x_sem.at[1], other)
+    mine[...] = in_ref[...]
+    copy.wait()
+    mine[total - 8 :, :] = in_ref[total - 8 :, :] + x_in[...]
+
+    copies = [remote(mine.at[rows_of(lax.rem(shard + k, 4))], y_in.at[k - 1], a_send.at[k - 1], a_recv.at[k - 1],
+                     shard_peer(k)) for k in range(1, 4)]
+    for copy in copies:
+        copy.wait()
+    z_in[ctx] = mine[rows_of(shard), :] + y_in[0] + y_in[1] + y_in[2]
+    copies = [remote(z_in.at[ctx], z_in.at[ctx], b_send.at[k - 1], b_recv.at[k - 1], ctx_peer(k))
+              for k in range(1, 4)]
+    for copy in copies:
+        copy.wait()
+    out_ref[rows_of(shard), :] = (z_in[0] + z_in[1]) + (z_in[2] + z_in[3])
+    copies = [remote(out_ref.at[rows_of(shard)], out_ref.at[rows_of(shard)], c_send.at[k - 1], c_recv.at[k - 1],
+                     shard_peer(k)) for k in range(1, 4)]
+    for copy in copies:
+        copy.wait()
+
+
+def small_sum(value):
+    rows, width = value.shape
+    quarter = rows // 4
+    vmem = pl.BlockSpec(memory_space=pltpu.VMEM)
+    three = pltpu.SemaphoreType.DMA((3,))
+    return pl.pallas_call(
+        small_kernel,
+        in_specs=[vmem],
+        out_specs=vmem,
+        out_shape=jax.ShapeDtypeStruct(value.shape, value.dtype),
+        scratch_shapes=[pltpu.VMEM((8, width), value.dtype), pltpu.VMEM(value.shape, value.dtype),
+                        pltpu.VMEM((3, quarter, width), value.dtype), pltpu.VMEM((4, quarter, width), value.dtype),
+                        pltpu.SemaphoreType.DMA((2,))] + [three] * 6,
+        compiler_params=pltpu.CompilerParams(collective_id=3, has_side_effects=True, vmem_limit_bytes=32 * 2**20),
+        cost_estimate=pl.CostEstimate(flops=0, bytes_accessed=40_000_000, transcendentals=0),
+        name="small_sum",
+    )(value)
 
 
 from jax.sharding import PartitionSpec as P
@@ -296,15 +646,43 @@
 
 
 def exchange_ends(last, total, back, axis):
-    devices, here = lax.axis_size(axis), lax.axis_index(axis)
-    everything = lax.all_gather(jnp.stack([last, total, back]), axis)
-    state = jnp.zeros_like(last)
-    for k in range(devices - 1):
-        state = jnp.where(k < here, everything[k, 1] * state + everything[k, 0], state)
-    adjoint = jnp.zeros_like(last)
-    for k in reversed(range(1, devices)):
-        adjoint = jnp.where(k > here, everything[k, 1] * adjoint + everything[k, 2], adjoint)
+    devices = lax.axis_size(axis)
+    state, adjoint = jnp.zeros_like(last), jnp.zeros_like(last)
+    ahead = jnp.stack([last, total]).astype(BF16)
+    behind = jnp.stack([back, total]).astype(BF16)
+    before = [from_behind(ahead, axis, k) for k in range(1, devices)]
+    after = [from_behind(behind, axis, -k) for k in range(1, devices)]
+    for part in reversed(before):
+        state = part[1].astype(jnp.float32) * state + part[0].astype(jnp.float32)
+    for part in reversed(after):
+        adjoint = part[1].astype(jnp.float32) * adjoint + part[0].astype(jnp.float32)
     return state, adjoint
+
+
+def group_rows(normed, g_mix, masks, fast):
+    modes, tokens = masks.shape
+    count = lax.axis_size("shard")
+    width = normed.shape[1]
+    deep = width // count
+    if not fast:
+        both = lax.all_to_all(jnp.stack([normed, g_mix]), "shard", 2, 1, tiled=True)
+        flags = lax.all_gather(masks, "shard", axis=1, tiled=True)
+        return jnp.stack([(both[0] * flags[index][:, None]).T for index in range(modes)] + [both[1].T])
+    flags = jnp.broadcast_to(jnp.pad(masks, ((0, 16 - modes), (0, 0))), (count, 16, tokens))
+    bundle = jnp.concatenate(
+        [normed.T.reshape(count, deep, tokens), g_mix.T.reshape(count, deep, tokens), flags], axis=1
+    )
+    here = lax.axis_index("shard")
+    whole = jnp.zeros((2 * deep + 16, count * tokens), BF16)
+    for k in range(count):
+        piece = lax.dynamic_index_in_dim(bundle, here ^ k, 0, keepdims=False)
+        if k:
+            piece = lax.ppermute(piece, "shard", [(i, i ^ k) for i in range(count)])
+        whole = lax.dynamic_update_slice(whole, piece, (0, (here ^ k) * tokens))
+    flags = whole[2 * deep :]
+    return jnp.stack(
+        [whole[:deep] * flags[index : index + 1] for index in range(modes)] + [whole[deep : 2 * deep]]
+    )
 
 
 def per_device(
@@ -330,12 +708,17 @@
     states = decay_log.shape[0]
     reach = filter_weight.shape[0] - 1
     rows = seqs * local_len
-    full_out = lax.all_gather(out_weight, "shard", axis=1, tiled=True)
-    full_in = lax.all_gather(in_weight, "shard", axis=1, tiled=True)
+    tps = lax.axis_size("tp")
+    modes, depth = in_weight.shape[:2]
+    in_own = in_weight.transpose(2, 0, 1, 3)
+    fast = (lax.axis_size("shard"), lax.axis_size("ctx"), lax.axis_size("tp")) == (4, 4, 2)
+    if fast:
+        conv_weight, gate_weight, full_out = gather_weights(in_own, out_weight)
+    else:
+        conv_weight, gate_weight = lax.all_gather(in_own, "shard", axis=2, tiled=True)
+        full_out = lax.all_gather(out_weight, "shard", axis=1, tiled=True)
     full_select = lax.all_gather(select_weight, "shard", axis=1, tiled=True)
     full_delta = lax.all_gather(delta_weight, "shard", axis=1, tiled=True)
-    modes = full_in.shape[0]
-    full_in = full_in.reshape(modes, width, 2 * inner)
     rank = full_delta.shape[1]
     mode_rows = modality.reshape(rows)
     masks = jnp.stack([(mode_rows == index).astype(BF16)[:, None] for index in range(modes)])
@@ -357,9 +740,18 @@
     whole = lax.all_gather(stream, "tp", axis=2, tiled=True).reshape(rows, width).astype(jnp.float32)
     inverse = lax.rsqrt(jnp.mean(whole * whole, axis=1, keepdims=True) + EPSILON)
     normed = (whole * inverse * norm_gain).astype(BF16)
-    projected = apply_modes(normed, full_in, 0)
-    conv_in = projected[:, :inner].astype(BF16).reshape(seqs, local_len, inner)
-    gate_in = projected[:, inner:]
+    normed_modes = jnp.concatenate([normed * masks[index] for index in range(modes)], axis=1)
+    conv_in = product(normed_modes, conv_weight.reshape(modes * width, inner), 1, 0)
+    conv_in = conv_in.astype(BF16).reshape(seqs, local_len, inner)
+    gate_in = product(normed_modes, gate_weight.reshape(modes * width, inner), 1, 0)
+    x = group_rows(normed, g_mix, masks[:, :, 0], fast)
+
+    def terms_of(lefts, grads):
+        return jnp.stack([product(left, grads, 1, 0) for left in lefts]).astype(BF16)
+
+    def summed(terms):
+        return lax.psum_scatter(terms, "ctx", scatter_dimension=1, tiled=True).astype(jnp.float32)
+
     edge = from_behind(conv_in[:, local_len - reach :], "ctx", 1)
     extended = jnp.concatenate([edge, conv_in], axis=1).astype(jnp.float32)
     offset = lax.axis_index("ctx") * local_len
@@ -386,14 +778,26 @@
     neg_decay = -jnp.exp(decay_log)
     _, blocks, groups = sizes(raw, seqs, states)
     a2 = state_form(neg_decay * LOG2E, blocks, groups)
-    ends = scan_ends(raw, conv_out, gate_in, g_gated, a2, b_in, c_out, cut, seqs)
-    carried, behind = exchange_ends(*ends, "ctx")
-    gated, g_gate, g_raw, g_conv, g_neg, g_b, g_c, g_skip = scan_both(
-        raw, conv_out, gate_in, g_gated, skip_gain, a2, carried, behind, b_in, c_out, cut, seqs
-    )
-
-    out_terms = product(gated, g_mix, 0, 0).astype(BF16)
-    out_grad = lax.psum_scatter(out_terms, ("shard", "ctx"), scatter_dimension=1, tiled=True)
+    ends = [scan_ends(raw, conv_out, gate_in, g_gated, a2[j], b_in, c_out, cut, seqs, j) for j in range(blocks)]
+    entering = [exchange_ends(*part, "ctx") for part in ends]
+    entering[0], ends[-1], x = lax.optimization_barrier((entering[0], ends[-1], x))
+    results = [
+        scan_both(raw, conv_out, gate_in, g_gated, skip_gain, a2[j], *entering[j], b_in, c_out, cut, seqs, j)
+        for j in range(blocks)
+    ]
+    early = []
+    for part in results[: 1 if fast else blocks]:
+        gate_all = lax.all_gather(part[1], "shard", axis=0, tiled=True)
+        gated_all = lax.all_gather(part[0], "shard", axis=0, tiled=True)
+        early.append((terms_of(x[:modes], gate_all), terms_of(x[modes:], gated_all)))
+    early, results = lax.optimization_barrier((early, results))
+    gate_grads = [summed(part[0]) for part in early]
+    out_grads = [summed(part[1])[0] for part in early]
+    gated, g_gate, g_raw, g_conv, g_neg, g_b, g_c, g_skip = zip(*results)
+    gated, g_gate, g_raw, g_conv = (jnp.concatenate(part, axis=1) for part in (gated, g_gate, g_raw, g_conv))
+    g_skip = jnp.concatenate(g_skip, axis=2)
+    g_neg = jnp.stack([jnp.sum(part, axis=0) for part in g_neg])
+
     mix_local = (
         lax.psum_scatter(
             product(gated, full_out, 1, 0).astype(BF16), "tp", scatter_dimension=1, tiled=True
@@ -402,15 +806,14 @@
     )
     local_stream = stream.reshape(rows, part_width).astype(jnp.float32)
     output = (local_stream + mix_local).astype(BF16).reshape(seqs, local_len, part_width)
-    stream_sq = jnp.sum(valid_rows * local_stream * local_stream)
-    mixer_sq = jnp.sum(mix_local * mix_local)
+    stream_sq = jnp.sum(valid_rows * jnp.sum(whole * whole, axis=1, keepdims=True))
     count = jnp.sum(valid_rows)
     skip_grad = jnp.sum(g_skip, axis=(0, 1))
-    decay_grad = from_state_form(jnp.sum(g_neg, axis=0)) * neg_decay
+    decay_grad = from_state_form(g_neg) * neg_decay
     bias_grad = product(masks[:, :, 0], g_raw, 1, 0)
     delta_terms = modal_terms(delta_low, g_raw)
     g_low = apply_modes(g_raw, full_delta, 1)
-    select_part = jnp.concatenate([g_low, pair_sum(g_b, states), pair_sum(g_c, states)], axis=1)
+    select_part = jnp.concatenate([g_low, pair_sum(sum(g_b), states), pair_sum(sum(g_c), states)], axis=1)
     g_sel_low = lax.psum(select_part, "tp").astype(BF16)
     select_terms = modal_terms(g_sel_low, conv_out)
     g_conv = g_conv + apply_modes(g_sel_low, full_select, 0)
@@ -426,45 +829,72 @@
     filter_grad = jnp.stack(filter_rows)
     returned = from_behind(g_ext[:, :reach], "ctx", -1)
     g_conv_in = g_ext[:, reach:] + jnp.pad(returned, ((0, 0), (local_len - reach, 0), (0, 0)))
-    g_projected = jnp.concatenate([g_conv_in.reshape(rows, inner).astype(BF16), g_gate], axis=1)
-    in_terms = modal_terms(normed, g_projected).astype(BF16).reshape(modes, width, 2, inner)
-    in_grad = lax.psum_scatter(in_terms, ("shard", "ctx"), scatter_dimension=1, tiled=True)
-    select_grad = lax.psum_scatter(select_terms, ("shard", "ctx"), scatter_dimension=1, tiled=True)
-    delta_grad = lax.psum_scatter(delta_terms, ("shard", "ctx"), scatter_dimension=1, tiled=True)
-
-    g_normed_part = apply_modes(g_projected, full_in, 1)
-    row_part = jnp.sum(g_normed_part * norm_gain * whole, axis=1, keepdims=True)
-    row_total = lax.psum(row_part, "tp")
+    g_conv_in = g_conv_in.reshape(rows, inner).astype(BF16)
+    if fast:
+        final = finish_weights(x, results[1][1], g_conv_in, results[1][0])
+        gate_grads.append(final[0:2])
+        conv_grad = jnp.concatenate([final[2:4], final[4:6]], axis=2)
+        out_grads.append(final[6])
+    else:
+        conv_grad = summed(terms_of(x[:modes], lax.all_gather(g_conv_in, "shard", axis=0, tiled=True)))
+    in_grad = jnp.stack([conv_grad, jnp.concatenate(gate_grads, axis=2)], axis=2)
+    out_grad = jnp.concatenate(out_grads, axis=1).T
+    group = lax.axis_size("shard") * lax.axis_size("ctx")
+    terms = jnp.concatenate(
+        [delta_terms.reshape(modes * group, -1, inner), select_terms.reshape(modes * group, -1, inner)], axis=1
+    ).astype(BF16)
+    terms = terms.reshape(modes, group, -1, inner).transpose(1, 0, 2, 3).reshape(group, -1, inner)
+    terms = jnp.pad(terms, ((0, 0), (0, -terms.shape[1] % 16), (0, 0)))
+    terms = lax.psum_scatter(terms, ("shard", "ctx"), scatter_dimension=0, tiled=True)[0].astype(jnp.float32)
+    deep = rank // group
+    terms = terms[: modes * (terms.shape[0] // modes)]
+    each = deep + full_select.shape[1] // group
+    terms = terms[: modes * each].reshape(modes, each, inner)
+    delta_grad, select_grad = terms[:, :deep], terms[:, deep:]
+
+    g_normed_part = sum(
+        product(grad * masks[index], weight[index], 1, 1)
+        for weight, grad in ((conv_weight, g_conv_in), (gate_weight, g_gate))
+        for index in range(modes)
+    )
+    row_total = lax.psum(jnp.sum(g_normed_part * norm_gain * whole, axis=1, keepdims=True), "tp")
+    gain_part = jnp.sum(g_normed_part * whole * inverse, axis=0)
+    scalars = jnp.stack([stream_sq * (1.0 / tps), jnp.sum(mix_local * mix_local), count * (1.0 / tps)])
+    small = jnp.concatenate([bias_grad, decay_grad, skip_grad[None], filter_grad, offset_grad[None]], axis=0)
+    if fast and width == inner and small.shape[0] == 24:
+        wide = jnp.stack([gain_part, jnp.pad(scalars, (0, width - 3))])
+        sums = small_sum(jnp.concatenate([small, jnp.pad(wide, ((0, 6), (0, 0)))], axis=0))
+        small_total, gain_total, scalars = sums[:24], sums[24], sums[25, :3]
+    else:
+        small_total = lax.psum(small, ("shard", "ctx"))
+        wide = lax.psum(jnp.concatenate([gain_part, scalars]), ("shard", "ctx", "tp"))
+        gain_total, scalars = wide[:width], wide[width:]
     g_normed = lax.psum_scatter(
         g_normed_part.astype(BF16), "tp", scatter_dimension=1, tiled=True
     ).astype(jnp.float32)
     start = lax.axis_index("tp") * part_width
     own_gain = lax.dynamic_slice_in_dim(norm_gain, start, part_width, 0)
     g_stream = inverse * own_gain * g_normed - local_stream * inverse**3 * row_total / width
-    gain_grad = jnp.sum(g_normed * local_stream * inverse, axis=0)
+    gain_grad = lax.dynamic_slice_in_dim(gain_total, start, part_width, 0)
     upstream_local = upstream.reshape(rows, part_width).astype(jnp.float32)
     stream_gradient = (upstream_local + g_stream).astype(BF16).reshape(seqs, local_len, part_width)
 
-    sums = lax.psum(
-        (gain_grad, bias_grad, filter_grad, offset_grad, decay_grad, skip_grad, count), ("shard", "ctx")
-    )
-    squares = lax.psum((stream_sq, mixer_sq), ("shard", "ctx", "tp"))
-    denominator = jnp.maximum(sums[6], 1.0) * width
-    stream_rms = jnp.sqrt(squares[0] / denominator)
-    mixer_rms = jnp.sqrt(squares[1] / denominator)
+    denominator = jnp.maximum(scalars[2], 1.0) * width
+    stream_rms = jnp.sqrt(scalars[0] / denominator)
+    mixer_rms = jnp.sqrt(scalars[1] / denominator)
     return (
         output,
         stream_gradient,
-        sums[0],
-        in_grad.astype(jnp.float32),
+        gain_grad,
+        in_grad,
         select_grad,
         delta_grad,
-        sums[1],
-        out_grad.astype(jnp.float32),
-        sums[2],
-        sums[3],
-        sums[4],
-        sums[5],
+        small_total[:modes],
+        out_grad,
+        small_total[modes + states + 1 : modes + states + 2 + reach],
+        small_total[modes + states + 2 + reach],
+        small_total[modes : modes + states],
+        small_total[modes + states],
         stream_rms,
         mixer_rms,
     )

time: 1360 us -> 854 us (0.63)
  waiting for transfers between devices: 747 us -> 24 us
  Pallas kernels: 129 us -> 491 us
  blocking collectives: 120 us -> 14.8 us
  local copies, waits for them, and re-layouts: 109 us -> 78.8 us
  starting transfers between devices: 6.3 us -> 29.9 us
  other arithmetic: 80.9 us -> 64.2 us
  matrix products: 135 us -> 120 us
    reduce_scatter x2 -> x3, waiting for transfers between devices: 393 us -> 0.02 us  [the longest x2 0.02 us: summed(): lax.psum_scatter(terms, 'ctx', scatter_dimension=1, tiled=True)]
    pallas_call x2 -> x7, Pallas kernels: 129 us -> 491 us  [the longest x1 190 us: finish_weights(): pl.pallas_call(finish_kernel, in_specs=[vmem, any_space, any_space, any_s...]
    all_gather x3 -> x2, waiting for transfers between devices: 268 us -> 0.04 us  [the longest x1 0.02 us: per_device(): gated_all = lax.all_gather(part[0], 'shard', axis=0, tiled=True)]
    psum x3 -> x1, blocking collectives: 109 us -> 4.25 us  [per_device(): lax.psum(jnp.sum(g_normed_part * norm_gain * whole, axis=1, keepdims=True...]
    all_gather x1, waiting for transfers between devices: 33.9 us -> 0.01 us  [per_device(): lax.all_gather(stream, 'tp', axis=2, tiled=True).reshape(rows, width)]
    unnamed x122 -> x168, local copies, waits for them, and re-layouts: 64.3 us -> 36.3 us
    slice x3 -> x9, local copies, waits for them, and re-layouts: 30.8 us -> 7.78 us  [the longest x1 3.1 us: per_device(): conv_grad = jnp.concatenate([final[2:4], final[4:6]], axis=2)]
    ppermute x2 -> x14, starting transfers between devices: 5.1 us -> 26.1 us  [from_behind(): return lax.ppermute(value, axis, pairs)]
  transfers between devices with their start and end apart: 16 -> 29, of which waited for: 11 -> 10; matrix products, arithmetic and copies ran while one was open for 21% -> 27% of each run, Pallas kernels for 0% -> 52%
where the time goes in v1:
time: 854 us; the launch traced here: 844 us
  Pallas kernels  491 us (57%)
  matrix products  120 us (14%)
  local copies, waits for them, and re-layouts  78.8 us (9%)
  other arithmetic  64.2 us (8%)
  starting transfers between devices  29.9 us (4%)
  waiting for transfers between devices  24 us (3%)
  between operations  21.6 us (3%)
  blocking collectives  14.8 us (2%)
    pallas_call x1, Pallas kernels, finish_weights(): pl.pallas_call(finish_kernel, in_specs=[vmem, any_space, any_space, any_s...  190 us
    pallas_call x1, Pallas kernels, gather_weights(): pl.pallas_call(functools.partial(gather_kernel, chunks), in_specs=[vmem]...  144 us
    dot_general x24, matrix products, product(): lax.dot_general(left, right, (((left_dim,), (right_dim,)), ((), ())), pre...  120 us
    pallas_call x2, Pallas kernels, scan_both(): pl.pallas_call(functools.partial(scan_kernel, groups, states, states, sta...  100 us
    pallas_call x2, Pallas kernels, scan_ends(): pl.pallas_call(functools.partial(ends_kernel, groups, states, states), gr...  36.4 us
    unnamed x168, local copies, waits for them, and re-layouts  36.3 us
    ppermute x14, starting transfers between devices, from_behind(): return lax.ppermute(value, axis, pairs)  26.1 us
    pallas_call x1, Pallas kernels, small_sum(): pl.pallas_call(small_kernel, in_specs=[vmem], out_specs=vmem, out_shape=j...  20.4 us
  transfers between devices with their start and end apart: 29, of which 10 were waited for; matrix products, arithmetic and copies ran while one was open for 27% of the time, Pallas kernels for 52%

profile of v1, /device:TPU:1, one launch (start us, length us, event | category | flops | bytes accessed | tf_op | source)
XLA Modules:
  0.0 843.9 jit_solution(16315236608575690559)
XLA Ops:
  11.1 10.8 %copy.108 = bf16[2,512,2,2048]{3,1,0,2:T(8,128)(2,1)} copy(bf16[2,512,2,2048]{3,2,1,0:T(2,128)(2,1)} %param.17) | data formatting | bytes 16777216 | tf_op args[2]
  26.3 143.7 %gather_weights.1 = (bf16[2,2048,2048]{2,1,0:T(8,128)(2,1)}, bf16[2,2048,2048]{2,1,0:T(8,128)(2,1)}, bf16[2048,2048]{1,0:T(8,128)(2,1)S(1)}) custom-call(bf16[2,512,2048]{2,1,0:T(8,128)(2,1)S(1)} %get-tuple-element.190.conv_ref, bf16[2,512,2048]{2,1,0:T(8,128)(2,1)S(1)} %get-tuple-element.189.gate_ref, bf16[2048,512]{1,0:T(8,128)(2,1)S(1)} %copy-done), custom_call_target="tpu_custom_call" | custom-call | bytes 400000000 | tf_op jit(solution)/shard_map/gather_weights/pallas_call | solution.py:364
  179.9 13.2 %convolution_convert_fusion.1 = bf16[512,2048]{1,0:T(8,128)(2,1)S(1)} fusion(bf16[4096,2048]{1,0:T(8,128)(2,1)} %bitcast.331, bf16[512,2048]{1,0:T(8,128)(2,1)S(1)} %broadcast_multiply_fusion.5, bf16[512,2048]{1,0:T(8,128)(2,1)S(1)} %get-tuple-element.187), kind=kOutput, calls=%fused_computation.47 | convolution fusion | flops 8599371776 | bytes 23068672 | tf_op jit(solution)/shard_map/dot_general | solution.py:643
  197.2 5.6 broadcast_multiply_fusion.2
  229.8 14.3 %fusion.21.gate_ref = f32[512,2048]{1,0:T(8,128)} fusion(bf16[4096,2048]{1,0:T(8,128)(2,1)} %bitcast.332, bf16[512,2048]{1,0:T(8,128)(2,1)S(1)} %copy-done.27, bf16[512,2048]{1,0:T(8,128)(2,1)S(1)} %copy-done.25), kind=kOutput, calls=%fused_computation.48 | convolution fusion | flops 8598323200 | bytes 25165824 | tf_op jit(solution)/shard_map/dot_general | solution.py:643
  244.2 6.2 fusion.112.gg_ref
  259.9 18.2 %scan_ends.2 = (f32[2,16,8,128]{3,2,1,0:T(8,128)}, f32[2,16,8,128]{3,2,1,0:T(8,128)}, f32[2,16,8,128]{3,2,1,0:T(8,128)}) custom-call(f32[512,2048]{1,0:T(8,128)} %add_add_fusion.1.raw_ref, bf16[512,2048]{1,0:T(8,128)(2,1)} %bitcast.257, f32[512,2048]{1,0:T(8,128)} %fusion.21.gate_ref, f32[512,2048]{1,0:T(8,128)} %fusion.112.gg_ref, ...), custom_call_target="tpu_custom_call" | custom-call | flops 67108864 | bytes 8388608 | tf_op jit(solution)/shard_map/scan_ends/pallas_call | solution.py:229
  290.7 5.0 collective-permute-done.5
  301.8 18.2 %scan_ends.3 = (f32[2,16,8,128]{3,2,1,0:T(8,128)}, f32[2,16,8,128]{3,2,1,0:T(8,128)}, f32[2,16,8,128]{3,2,1,0:T(8,128)}) custom-call(f32[512,2048]{1,0:T(8,128)} %add_add_fusion.1.raw_ref, bf16[512,2048]{1,0:T(8,128)(2,1)} %bitcast.258, f32[512,2048]{1,0:T(8,128)} %fusion.21.gate_ref, f32[512,2048]{1,0:T(8,128)} %fusion.112.gg_ref, ...), custom_call_target="tpu_custom_call" | custom-call | flops 67108864 | bytes 8388608 | tf_op jit(solution)/shard_map/scan_ends/pallas_call | solution.py:229
  341.0 50.0 %scan_both.2 = (bf16[512,1024]{1,0:T(8,128)(2,1)}, bf16[512,1024]{1,0:T(8,128)(2,1)}, bf16[512,1024]{1,0:T(8,128)(2,1)}, f32[512,1024]{1,0:T(8,128)}, f32[2,16,8...) custom-call(f32[512,2048]{1,0:T(8,128)} %add_add_fusion.1.raw_ref, ...), custom_call_target="tpu_custom_call" | custom-call | flops 184549376 | bytes 16777216 | tf_op jit(solution)/shard_map/scan_both/pallas_call | solution.py:256
  395.8 6.7 collective-permute-start.12
  411.1 50.0 %scan_both.3 = (bf16[512,1024]{1,0:T(8,128)(2,1)}, bf16[512,1024]{1,0:T(8,128)(2,1)}, bf16[512,1024]{1,0:T(8,128)(2,1)}, f32[512,1024]{1,0:T(8,128)}, f32[2,16,8...) custom-call(f32[512,2048]{1,0:T(8,128)} %add_add_fusion.1.raw_ref, ...), custom_call_target="tpu_custom_call" | custom-call | flops 184549376 | bytes 16777216 | tf_op jit(solution)/shard_map/scan_both/pallas_call | solution.py:256
  461.2 5.3 fusion.62
  472.1 6.3 fusion.59
  482.6 10.6 %all-reduce.14 = bf16[512,160]{0,1:T(8,128)(2,1)S(1)} all-reduce(f32[512,160]{0,1:T(8,128)S(1)} %pad_maximum_fusion.7), channel_id=1, replica_groups=mesh['shard'=4,'ctx'=4,'tp'=2] {'tp'}, use_global_device_ids=true, to_apply=%region_5.6 | all-reduce | flops 81920 | bytes 491520 | tf_op jit(solution)/shard_map/psum | solution.py:817
  513.4 10.8 %fusion = f32[512,2048]{1,0:T(8,128)} fusion(bf16[2,2048,2048]{2,1,0:T(8,128)(2,1)} %get-tuple-element.61, bf16[512,2048]{1,0:T(8,128)(2,1)} %constant_dynamic-update-slice_fusion.2, bf16[512]{0:T(512)(128)(2,1)S(1)} %bitcast.294), kind=kOutput, calls=%fused_computation | convolution fusion | flops 4296015872 | bytes 14681088 | tf_op jit(solution)/shard_map/dot_general | solution.py:643
  524.2 10.2 %fusion.2 = f32[512,2048]{1,0:T(8,128)} fusion(bf16[2,2048,2048]{2,1,0:T(8,128)(2,1)} %get-tuple-element.61, bf16[512,2048]{1,0:T(8,128)(2,1)S(1)} %copy-done.36, bf16[512]{0:T(512)(128)(2,1)S(1)} %bitcast.301), kind=kOutput, calls=%fused_computation.2 | convolution fusion | flops 4296015872 | bytes 14681088 | tf_op jit(solution)/shard_map/dot_general | solution.py:643
  534.4 5.8 convolution_convert_fusion
  540.2 10.5 %pad_add_fusion = f32[2,259,2048]{2,1,0:T(8,128)} fusion(f32[2,256,2048]{2,1,0:T(8,128)} %copy-done.4, f32[2,256,2048]{2,1,0:T(8,128)} %copy-done.5, f32[2,256,2048]{2,1,0:T(8,128)} %copy-done.6, f32[2,256,2048]{2,1,0:T(8,128)} %copy-done.3), kind=kLoop, calls=%fused_computation.14 | loop fusion | flops 3182592 | bytes 21020672 | tf_op jit(solution)/shard_map/add | solution.py:828
  555.7 9.7 %fusion.4 = f32[512,2048]{1,0:T(8,128)} fusion(bf16[512,2048]{1,0:T(8,128)(2,1)S(1)} %bitcast.274, bf16[2,2048,2048]{2,1,0:T(8,128)(2,1)} %get-tuple-element.60), kind=kOutput, calls=%fused_computation.4 | convolution fusion | flops 4294967296 | bytes 14680064 | tf_op jit(solution)/shard_map/dot_general | solution.py:643
  565.4 13.3 %fusion.18 = (f32[2048]{0:T(1024)S(1)}, f32[512]{0:T(512)S(1)}, bf16[512,2048]{1,0:T(8,128)(2,1)}) fusion(bf16[2,256,2048]{2,1,0:T(8,128)(2,1)S(1)} %copy-done.17, f32[512]{0:T(512)S(1)} %bitcast.305, f32[2048]{0:T(1024)S(1)} %copy-done.58, f32[512,2048]{1,0:T(8,128)} %fusion, f32[512,2048]{1,0:T(8,128)} %fusion.2, f32[512,2048]{1,0:T(8,128)} %fusion.4, ...), kind=kOutput, calls=%fused_computation.32 | convolution fusion | flops 4306499072 | bytes 27283456 | tf_op jit(solution)/shard_map/dot_general | solution.py:643
  593.3 190.3 %finish_weights.1 = f32[7,128,1024]{2,1,0:T(8,128)} custom-call(bf16[3,512,2048]{2,1,0:T(8,128)(2,1)} %pad_maximum_fusion.x_ref, bf16[512,1024]{1,0:T(8,128)(2,1)} %get-tuple-element.99.gate_ref, bf16[512,2048]{1,0:T(8,128)(2,1)} %bitcast.265, bf16[512,1024]{1,0:T(8,128)(2,1)} %get-tuple-element.89.gated_ref), custom_call_target="tpu_custom_call" | custom-call | flops 15032385536 | bytes 500000000 | tf_op jit(solution)/shard_map/finish_weights/pallas_call | solution.py:548
  795.3 5.2 copy.90
  806.1 20.4 %small_sum.1 = f32[32,2048]{1,0:T(8,128)S(1)} custom-call(f32[32,2048]{1,0:T(8,128)S(1)} %concatenate.70.in_ref), custom_call_target="tpu_custom_call" | custom-call | bytes 40000000 | tf_op jit(solution)/shard_map/small_sum/pallas_call | solution.py:616
  (361 shorter events, 182.2 us)
Async XLA Ops:
  7.2 166.1 %all-gather.7.cloned.1.call-start = ((), (), s32[]{:S(2)}) async-start(), calls=%async_computation.5 | async-start | bytes 3145728 | tf_op jit(solution)/shard_map/all_gather | solution.py:740
  7.9 196.6 %all-gather.9.cloned.1.call-start = ((), (), s32[]{:S(2)}) async-start(), calls=%async_computation.6 | async-start | bytes 1638400 | tf_op jit(solution)/shard_map/all_gather | solution.py:720
  8.7 204.0 %all-gather.13.cloned.1.call-start = ((), (), s32[]{:S(2)}) async-start(), calls=%async_computation.9 | async-start | bytes 3145728 | tf_op jit(solution)/shard_map/all_gather | solution.py:737
  9.4 241.0 %all-reduce.13.cloned.1.call-start = ((), (), s32[]{:S(2)}) async-start(), calls=%async_computation.7 | async-start | bytes 655360 | tf_op jit(solution)/shard_map/psum | solution.py:771
  210.5 44.5 %all-gather.11.cloned.1.call-start = ((), (), s32[]{:S(2)}) async-start(), calls=%async_computation.8 | async-start | bytes 1310720 | tf_op jit(solution)/shard_map/all_gather | solution.py:721
  211.1 250.1 %all-gather.15.cloned.1.call-start = ((), (), s32[]{:S(2)}) async-start(), calls=%async_computation.10 | async-start | bytes 5242880 | tf_op jit(solution)/shard_map/all_gather | solution.py:790
  228.8 98.7 %collective-permute-start.7 = (bf16[1040,512]{1,0:T(8,128)(2,1)}, bf16[1040,512]{1,0:T(8,128)(2,1)S(1)}, u32[]{:S(2)}, u32[]{:S(2)}) collective-permute-start(bf16[1040,512]{1,0:T(8,128)(2,1)} %get-tuple-element.196), channel_id=1, source_target_pairs={{0,8},{8,0},{16,24},{24,16},{1,9},{9,1},{17,25},{25,17},{2,10},{10... | collective-permute-start | bytes 3194888 | tf_op jit(solution)/shard_map/ppermute | solution.py:680
  280.9 8.5 %collective-permute-start.6 = (bf16[2,2,16,8,128]{4,3,2,1,0:T(8,128)(2,1)S(1)}, bf16[2,2,16,8,128]{4,3,2,1,0:T(8,128)(2,1)S(1)}, u32[]{:S(2)}, u32[]{:S(2)}) collective-permute-start(bf16[2,2,16,8,128]{4,3,2,1,0:T(8,128)(2,1)S(1)} %get-tuple-element.222), channel_id=1, source_target_pairs={{6,0},{7,1},{14,8},{15,9},{22,16},{23,17},{30,24},{31,25}} | collective-permute-start | bytes 393224 | tf_op jit(solution)/shard_map/ppermute | solution.py:639
  282.2 13.5 %collective-permute-start.5 = (bf16[2,2,16,8,128]{4,3,2,1,0:T(8,128)(2,1)S(1)}, bf16[2,2,16,8,128]{4,3,2,1,0:T(8,128)(2,1)S(1)}, u32[]{:S(2)}, u32[]{:S(2)}) collective-permute-start(bf16[2,2,16,8,128]{4,3,2,1,0:T(8,128)(2,1)S(1)} %get-tuple-element.222), channel_id=1, source_target_pairs={{4,0},{6,2},{5,1},{7,3},{12,8},{14,10},{13,9},{15,11},{20,16},{22,... | collective-permute-start | bytes 393224 | tf_op jit(solution)/shard_map/ppermute | solution.py:639
  283.5 45.1 %collective-permute-start.8 = (bf16[1040,512]{1,0:T(8,128)(2,1)}, bf16[1040,512]{1,0:T(8,128)(2,1)S(1)}, u32[]{:S(2)}, u32[]{:S(2)}) collective-permute-start(bf16[1040,512]{1,0:T(8,128)(2,1)} %get-tuple-element.195), channel_id=1, source_target_pairs={{0,16},{8,24},{16,0},{24,8},{1,17},{9,25},{17,1},{25,9},{2,18},{10... | collective-permute-start | bytes 3194888 | tf_op jit(solution)/shard_map/ppermute | solution.py:680
  283.6 48.3 %collective-permute-start.9 = (bf16[1040,512]{1,0:T(8,128)(2,1)}, bf16[1040,512]{1,0:T(8,128)(2,1)}, u32[]{:S(2)}, u32[]{:S(2)}) collective-permute-start(bf16[1040,512]{1,0:T(8,128)(2,1)} %get-tuple-element.194), channel_id=1, source_target_pairs={{0,24},{8,16},{16,8},{24,0},{1,25},{9,17},{17,9},{25,1},{2,26},{10... | collective-permute-start | bytes 3194888 | tf_op jit(solution)/shard_map/ppermute | solution.py:680
  289.4 30.6 %collective-permute-start.4 = (bf16[2,2,16,8,128]{4,3,2,1,0:T(8,128)(2,1)S(1)}, bf16[2,2,16,8,128]{4,3,2,1,0:T(8,128)(2,1)S(1)}, u32[]{:S(2)}, u32[]{:S(2)}) collective-permute-start(bf16[2,2,16,8,128]{4,3,2,1,0:T(8,128)(2,1)S(1)} %get-tuple-element.222), channel_id=1, source_target_pairs={{2,0},{4,2},{6,4},{3,1},{5,3},{7,5},{10,8},{12,10},{14,12},{11,9},... | collective-permute-start | bytes 393224 | tf_op jit(solution)/shard_map/ppermute | solution.py:639
  295.7 25.7 %collective-permute-start.3 = (bf16[2,2,16,8,128]{4,3,2,1,0:T(8,128)(2,1)S(1)}, bf16[2,2,16,8,128]{4,3,2,1,0:T(8,128)(2,1)S(1)}, u32[]{:S(2)}, u32[]{:S(2)}) collective-permute-start(bf16[2,2,16,8,128]{4,3,2,1,0:T(8,128)(2,1)S(1)} %get-tuple-element.223), channel_id=1, source_target_pairs={{0,6},{1,7},{8,14},{9,15},{16,22},{17,23},{24,30},{25,31}} | collective-permute-start | bytes 393224 | tf_op jit(solution)/shard_map/ppermute | solution.py:639
  391.0 81.1 %all-gather.17.cloned.1.call-start = ((), (), s32[]{:S(2)}) async-start(), calls=%async_computation.11 | async-start | bytes 5242880 | tf_op jit(solution)/shard_map/all_gather | solution.py:791
  391.7 397.1 %reduce-scatter.14.cloned.1.call-start = ((), (), s32[]{:S(2)}) async-start(), calls=%async_computation.16 | async-start | bytes 1310720 | tf_op jit(solution)/shard_map/reduce_scatter | solution.py:753
  391.9 11.9 %collective-permute-start.15 = (bf16[2,2,16,8,128]{4,3,2,1,0:T(8,128)(2,1)S(1)}, bf16[2,2,16,8,128]{4,3,2,1,0:T(8,128)(2,1)S(1)}, u32[]{:S(2)}, u32[]{:S(2)}) collective-permute-start(bf16[2,2,16,8,128]{4,3,2,1,0:T(8,128)(2,1)S(1)} %get-tuple-element.220), channel_id=1, source_target_pairs={{6,0},{7,1},{14,8},{15,9},{22,16},{23,17},{30,24},{31,25}} | collective-permute-start | bytes 393224 | tf_op jit(solution)/shard_map/ppermute | solution.py:639
  393.2 13.5 %collective-permute-start.14 = (bf16[2,2,16,8,128]{4,3,2,1,0:T(8,128)(2,1)S(1)}, bf16[2,2,16,8,128]{4,3,2,1,0:T(8,128)(2,1)S(1)}, u32[]{:S(2)}, u32[]{:S(2)}) collective-permute-start(bf16[2,2,16,8,128]{4,3,2,1,0:T(8,128)(2,1)S(1)} %get-tuple-element.220), channel_id=1, source_target_pairs={{4,0},{6,2},{5,1},{7,3},{12,8},{14,10},{13,9},{15,11},{20,16},{22,... | collective-permute-start | bytes 393224 | tf_op jit(solution)/shard_map/ppermute | solution.py:639
  394.5 12.2 %collective-permute-start.13 = (bf16[2,2,16,8,128]{4,3,2,1,0:T(8,128)(2,1)S(1)}, bf16[2,2,16,8,128]{4,3,2,1,0:T(8,128)(2,1)S(1)}, u32[]{:S(2)}, u32[]{:S(2)}) collective-permute-start(bf16[2,2,16,8,128]{4,3,2,1,0:T(8,128)(2,1)S(1)} %get-tuple-element.220), channel_id=1, source_target_pairs={{2,0},{4,2},{6,4},{3,1},{5,3},{7,5},{10,8},{12,10},{14,12},{11,9},... | collective-permute-start | bytes 393224 | tf_op jit(solution)/shard_map/ppermute | solution.py:639
  395.8 11.6 %collective-permute-start.12 = (bf16[2,2,16,8,128]{4,3,2,1,0:T(8,128)(2,1)S(1)}, bf16[2,2,16,8,128]{4,3,2,1,0:T(8,128)(2,1)S(1)}, u32[]{:S(2)}, u32[]{:S(2)}) collective-permute-start(bf16[2,2,16,8,128]{4,3,2,1,0:T(8,128)(2,1)S(1)} %get-tuple-element.221), channel_id=1, source_target_pairs={{0,6},{1,7},{8,14},{9,15},{16,22},{17,23},{24,30},{25,31}} | collective-permute-start | bytes 393224 | tf_op jit(solution)/shard_map/ppermute | solution.py:639
  478.4 313.9 %reduce-scatter.10.cloned.1.call-start = ((), (), s32[]{:S(2)}) async-start(), calls=%async_computation.14 | async-start | bytes 2621440 | tf_op jit(solution)/shard_map/reduce_scatter | solution.py:753
  509.7 41.5 %collective-permute-start.16 = (f32[2,3,2048]{2,1,0:T(4,128)S(1)}, f32[2,3,2048]{2,1,0:T(4,128)S(1)}, u32[]{:S(2)}, u32[]{:S(2)}) collective-permute-start(f32[2,3,2048]{2,1,0:T(4,128)S(1)} %pad_add_fusion.1), channel_id=1, source_target_pairs={{2,0},{4,2},{6,4},{3,1},{5,3},{7,5},{10,8},{12,10},{14,12},{11,9},... | collective-permute-start | bytes 147464 | tf_op jit(solution)/shard_map/ppermute | solution.py:639
  512.3 288.3 %reduce-scatter.6.cloned.1.call-start = ((), (), s32[]{:S(2)}) async-start(), calls=%async_computation.12 | async-start | bytes 3145728 | tf_op jit(solution)/shard_map/reduce_scatter | solution.py:802
  550.7 249.8 %reduce-scatter.8.cloned.1.call-start = ((), (), s32[]{:S(2)}) async-start(), calls=%async_computation.13 | async-start | bytes 3145728 | tf_op jit(solution)/shard_map/reduce_scatter | solution.py:872
  578.7 253.5 %reduce-scatter.12.cloned.1.call-start = ((), (), s32[]{:S(2)}) async-start(), calls=%async_computation.15 | async-start | bytes 3342336 | tf_op jit(solution)/shard_map/reduce_scatter | solution.py:848
  (84 other events, 1656.6 us)
Sparse Core Ops, SparseCore 0:
  9.6 35.1 all-gather.6
  46.3 25.7 all-gather.8
  73.7 32.7 all-gather.12
  210.6 25.6 all-reduce.12
  237.7 17.1 all-gather.10
  391.1 35.2 all-gather.14
  428.0 34.4 all-gather.16
  478.5 30.5 reduce-scatter.13
  512.4 51.3 reduce-scatter.9
  565.9 31.2 reduce-scatter.5
  599.5 31.7 reduce-scatter.7
  635.4 83.7 reduce-scatter.11

commit v2 on v1

--- a/solution.py
+++ b/solution.py
@@ -37,35 +37,142 @@
     lax.fori_loop(0, raw_ref.shape[0] // 16, step, 0)
 
 
-def ends_kernel(groups, states, split, raw_ref, conv_ref, gate_ref, gg_ref, a_ref, b_ref, c_ref,
+def ends_of(first, tokens, groups, states, a_ref, b_ref, c_ref, cut_ref, delta_s, conv_s, g_s):
+    def eight_tokens(tile, carry):
+        h, p, l = (list(part) for part in carry)
+        for i in range(8):
+            rows = pl.ds(tile * (groups * 8) + i, groups, stride=8)
+            delta = delta_s[rows, :]
+            signal = delta * conv_s[rows, :]
+            g = g_s[rows, :]
+            token = first + tile * 8 + i
+            reach = delta + cut_ref[token]
+            for n in range(states):
+                decay = jnp.exp2(reach * a_ref[n])
+                h[n] = decay * h[n] + signal * b_ref[token * states + n]
+                p[n] = decay * p[n]
+                l[n] = l[n] + p[n] * (g * c_ref[token * states + n])
+        return tuple(h), tuple(p), tuple(l)
+
+    zero = tuple(jnp.zeros((groups, 128), jnp.float32) for _ in range(states))
+    one = tuple(jnp.ones((groups, 128), jnp.float32) for _ in range(states))
+    return lax.fori_loop(0, tokens // 8, eight_tokens, (zero, one, zero))
+
+
+def ends_kernel(groups, states, raw_ref, conv_ref, gate_ref, gg_ref, a_ref, b_ref, c_ref,
                 cut_ref, h_ref, p_ref, l_ref, delta_s, conv_s, g_s):
     tokens = raw_ref.shape[0]
-    first = pl.program_id(0) * tokens
     stage_rows(raw_ref, conv_ref, gate_ref, gg_ref, delta_s, conv_s, g_s, groups)
-    for low in range(0, states, split):
-        names = range(low, low + split)
-
-        def eight_tokens(tile, carry):
-            h, p, l = (list(part) for part in carry)
-            for i in range(8):
-                rows = pl.ds(tile * (groups * 8) + i, groups, stride=8)
-                delta = delta_s[rows, :]
-                signal = delta * conv_s[rows, :]
-                g = g_s[rows, :]
-                token = first + tile * 8 + i
-                reach = delta + cut_ref[token]
-                for k, n in enumerate(names):
-                    decay = jnp.exp2(reach * a_ref[n])
-                    h[k] = decay * h[k] + signal * b_ref[token * states + n]
-                    p[k] = decay * p[k]
-                    l[k] = l[k] + p[k] * (g * c_ref[token * states + n])
-            return tuple(h), tuple(p), tuple(l)
-
-        zero = tuple(jnp.zeros((groups, 128), jnp.float32) for _ in names)
-        one = tuple(jnp.ones((groups, 128), jnp.float32) for _ in names)
-        h, p, l = lax.fori_loop(0, tokens // 8, eight_tokens, (zero, one, zero))
-        for k, n in enumerate(names):
-            h_ref[n], p_ref[n], l_ref[n] = h[k], p[k], l[k]
+    h, p, l = ends_of(pl.program_id(0) * tokens, tokens, groups, states, a_ref, b_ref, c_ref, cut_ref,
+                      delta_s, conv_s, g_s)
+    for n in range(states):
+        h_ref[n], p_ref[n], l_ref[n] = h[n], p[n], l[n]
+
+
+def entering_kernel(groups, states, seqs, raw_ref, conv_ref, gate_ref, gg_ref, a_ref, b_ref, c_ref, cut_ref,
+                    normed_ref, gmix_ref, flag_ref, h0_ref, q0_ref, normed_group, gmix_group, flag_group, delta_s,
+                    conv_s, g_s, ahead, behind, before, after, up_send, up_recv, down_send, down_recv, row_send,
+                    row_recv, stay_sem):
+    shard, ctx = lax.axis_index("shard"), lax.axis_index("ctx")
+    block, seq = pl.program_id(0), pl.program_id(1)
+    step = block * seqs + seq
+    steps = ahead.shape[0]
+    tokens = raw_ref.shape[0]
+    rows, deep = normed_ref.shape[0], normed_ref.shape[1] // 4
+
+    def remote(source, target, send_sem, recv_sem, to):
+        return pltpu.make_async_remote_copy(src_ref=source, dst_ref=target, send_sem=send_sem, recv_sem=recv_sem,
+                                            device_id=to, device_id_type=MESH)
+
+    def features(owner):
+        return pl.ds(pl.multiple_of(owner * deep, deep), deep)
+
+    def from_me():
+        mine = pl.ds(pl.multiple_of(shard * rows, rows), rows)
+        return normed_group.at[mine], gmix_group.at[mine], flag_group.at[:, mine]
+
+    def row_copies(k):
+        peer = lax.rem(shard + k, 4)
+        sources = (normed_ref.at[:, features(peer)], gmix_ref.at[:, features(peer)], flag_ref)
+        return [remote(s, t, row_send.at[k - 1, i], row_recv.at[k - 1, i], {"shard": peer})
+                for i, (s, t) in enumerate(zip(sources, from_me()))]
+
+    def stays():
+        sources = (normed_ref.at[:, features(shard)], gmix_ref.at[:, features(shard)], flag_ref)
+        return [pltpu.make_async_copy(s, t, stay_sem.at[i]) for i, (s, t) in enumerate(zip(sources, from_me()))]
+
+    def up(i, d):
+        return remote(ahead.at[i], before.at[d - 1, i], up_send.at[i, d - 1], up_recv.at[i, d - 1], {"ctx": ctx + d})
+
+    def down(i, d):
+        return remote(behind.at[i], after.at[d - 1, i], down_send.at[i, d - 1], down_recv.at[i, d - 1],
+                      {"ctx": ctx - d})
+
+    @pl.when(step == 0)
+    def _():
+        barrier = pltpu.get_barrier_semaphore()
+        for k in range(1, 4):
+            pl.semaphore_signal(barrier, inc=1, device_id={"shard": lax.rem(shard + k, 4)}, device_id_type=MESH)
+            pl.semaphore_signal(barrier, inc=1, device_id={"ctx": lax.rem(ctx + k, 4)}, device_id_type=MESH)
+        pl.semaphore_wait(barrier, 6)
+        for k in range(1, 4):
+            for copy in row_copies(k):
+                copy.start()
+        for copy in stays():
+            copy.start()
+        for d in range(1, 4):
+            @pl.when(ctx < d)
+            def _():
+                before[d - 1] = jnp.zeros(before.shape[1:], before.dtype)
+
+            @pl.when(ctx + d > 3)
+            def _():
+                after[d - 1] = jnp.zeros(after.shape[1:], after.dtype)
+
+    stage_rows(raw_ref, conv_ref, gate_ref, gg_ref, delta_s, conv_s, g_s, groups)
+    h, p, l = ends_of(seq * tokens, tokens, groups, states, a_ref, b_ref, c_ref, cut_ref, delta_s, conv_s, g_s)
+    for n in range(0, states, 2):
+        for k, values in enumerate((h, p)):
+            both = jnp.concatenate([values[n], values[n + 1]], axis=0).astype(ahead.dtype)
+            ahead[step, k, n * groups : (n + 2) * groups, :] = both
+        for k, values in enumerate((l, p)):
+            both = jnp.concatenate([values[n], values[n + 1]], axis=0).astype(behind.dtype)
+            behind[step, k, n * groups : (n + 2) * groups, :] = both
+
+    for d in range(1, 4):
+        @pl.when(ctx + d < 4)
+        def _():
+            up(step, d).start()
+
+        @pl.when(ctx >= d)
+        def _():
+            down(step, d).start()
+
+    @pl.when(step == steps - 1)
+    def _():
+        for d in range(1, 4):
+            for i in range(steps):
+                @pl.when(ctx >= d)
+                def _():
+                    up(i, d).wait_recv()
+                    down(i, d).wait_send()
+
+                @pl.when(ctx + d < 4)
+                def _():
+                    up(i, d).wait_send()
+                    down(i, d).wait_recv()
+
+        for i in range(steps):
+            for out, got in ((h0_ref, before), (q0_ref, after)):
+                total = got[2, i, 0].astype(jnp.float32)
+                for d in (1, 0):
+                    total = got[d, i, 1].astype(jnp.float32) * total + got[d, i, 0].astype(jnp.float32)
+                out[i] = total
+        for k in range(1, 4):
+            for copy in row_copies(k):
+                copy.wait()
+        for copy in stays():
+            copy.wait()
 
 
 def scan_kernel(groups, states, fsplit, bsplit, raw_ref, conv_ref, gate_ref, gg_ref, skip_ref, a_ref, h0_ref,
@@ -227,7 +334,7 @@
     out = jax.ShapeDtypeStruct((seqs, states, groups, 128), jnp.float32)
     elements = raw.shape[0] * width * states
     return pl.pallas_call(
-        functools.partial(ends_kernel, groups, states, states),
+        functools.partial(ends_kernel, groups, states),
         grid=(seqs,),
         in_specs=[token_spec(tokens, width, block)] * 4
         + [pl.BlockSpec((states, groups, 128), lambda s: (0, 0, 0)), smem, smem, smem],
@@ -373,19 +480,23 @@
     )(in_own[0], in_own[1], out_own)
 
 
-def finish_kernel(x_ref, gate_ref, conv_ref, gated_ref, sum_ref, blocks, part, below, above, y_send, y_recv,
-                  core_send, core_recv, pass_send, pass_recv, local_sem, up_send, up_recv, down_send, down_recv):
-    shard, ctx = lax.axis_index("shard"), lax.axis_index("ctx")
+def finish_kernel(x_ref, first_0, first_1, first_2, first_3, conv_ref, gated_ref, gate_ref, mask_ref, conv_weight,
+                  gate_weight, sum_ref, normed_ref, other_ref, blocks, part, came, gate_s, weight_s, give_s, y_send,
+                  y_recv, core_send, core_recv, pass_send, pass_recv, local_sem, first_sem, gate_sem, weight_sem,
+                  x_sem, up_send, up_recv, down_send, down_recv):
+    shard, ctx, tp = lax.axis_index("shard"), lax.axis_index("ctx"), lax.axis_index("tp")
     far = lax.rem(shard + 2, 4)
     core = {"shard": shard + 1 - 2 * lax.rem(shard, 2)}
     across = {"shard": far}
     jobs, units, last = blocks.shape[0], part.shape[0], 3
-    tokens, width = gate_ref.shape
-    deep = sum_ref.shape[1]
-    up, down = {"ctx": ctx + 1}, {"ctx": ctx - 1}
+    tokens, width = gated_ref.shape
+    deep, narrow = sum_ref.shape[1:]
+    up, down, beside = {"ctx": ctx + 1}, {"ctx": ctx - 1}, {"tp": 1 - tp}
+    features = weight_s.shape[3]
+    steps = normed_ref.shape[1] // features
 
     barrier = pltpu.get_barrier_semaphore()
-    for peer in (core, across):
+    for peer in (core, across, beside):
         pl.semaphore_signal(barrier, inc=1, device_id=peer, device_id_type=MESH)
 
     @pl.when(ctx < last)
@@ -396,9 +507,9 @@
     def _():
         pl.semaphore_signal(barrier, inc=1, device_id=down, device_id_type=MESH)
 
-    pl.semaphore_wait(barrier, 2 + jnp.where(ctx < last, 1, 0) + jnp.where(ctx > 0, 1, 0))
-
-    sources = [gate_ref, conv_ref.at[:, pl.ds(0, width)], conv_ref.at[:, pl.ds(width, width)], gated_ref]
+    pl.semaphore_wait(barrier, 3 + jnp.where(ctx < last, 1, 0) + jnp.where(ctx > 0, 1, 0))
+
+    sources = [None, conv_ref.at[:, pl.ds(0, width)], conv_ref.at[:, pl.ds(width, width)], gated_ref]
 
     def rows_of(owner):
         return pl.ds(pl.multiple_of(owner * tokens, tokens), tokens)
@@ -426,43 +537,71 @@
         if j + 2 < jobs:
             cross(j + 2).start()
 
-    def hop(u, k, buffer, send_sem, recv_sem, to):
+    def hop(u, k, slot, send_sem, recv_sem, to):
         rows = pl.ds(pl.multiple_of(k * deep, deep), deep)
-        return remote(part.at[u, rows], buffer.at[u, rows], send_sem.at[u, k], recv_sem.at[u, k], to)
+        there = pl.ds(pl.multiple_of(slot * deep, deep), deep)
+        return remote(part.at[u, rows], came.at[u, there], send_sem.at[u, k], recv_sem.at[u, k], to)
 
     def going_up(u, k):
-        return hop(u, k, below, up_send, up_recv, up)
+        return hop(u, k, k, up_send, up_recv, up)
 
     def going_down(u, k):
-        return hop(u, k, above, down_send, down_recv, down)
-
-    def add(u, k, buffer):
+        return hop(u, k, jnp.where(k == ctx - 1, last + 1, k), down_send, down_recv, down)
+
+    def coming_down(u, k):
+        return hop(u, k, jnp.where(k == ctx, last + 1, k), down_send, down_recv, down)
+
+    def add(u, k):
         rows = pl.ds(k * deep, deep)
-        total = part[u, rows, :].astype(jnp.float32) + buffer[u, rows, :].astype(jnp.float32)
+        total = part[u, rows, :].astype(jnp.float32) + came[u, rows, :].astype(jnp.float32)
         part[u, rows, :] = total.astype(part.dtype)
 
-    for j in range(min(2, jobs)):
+    def feature_rows(i):
+        return pl.multiple_of(lax.rem(i + (1 - tp) * (steps // 2), steps) * features, features)
+
+    def load(i, slot):
+        rows = pl.ds(feature_rows(i), features)
+        return [pltpu.make_async_copy(ref.at[:, rows], weight_s.at[slot, k], weight_sem.at[slot, k])
+                for k, ref in enumerate((conv_weight, gate_weight))]
+
+    def beside_copy():
+        return remote(give_s, other_ref, x_sem.at[0], x_sem.at[1], beside)
+
+    owners = (shard, shard + 1 - 2 * lax.rem(shard, 2), far, 3 - shard)
+    firsts = [pltpu.make_async_copy(ref, blocks.at[0, rows_of(owner)], first_sem.at[k])
+              for k, (owner, ref) in enumerate(zip(owners, (first_0, first_1, first_2, first_3)))]
+    for copy in firsts:
+        copy.start()
+    for j in range(1, min(3, jobs)):
         cross(j).start()
-    for j in range(jobs):
+    own_gate = pltpu.make_async_copy(gate_ref, gate_s, gate_sem.at[0])
+    own_gate.start()
+    for j in range(1, jobs):
         stay(j).start()
         pair(j).start()
-    advance(0)
+    for copy in load(0, 0):
+        copy.start()
+    for copy in firsts:
+        copy.wait()
+    own_gate.wait()
+    for j in range(1, jobs):
+        stay(j).wait()
 
     def step(t, _):
-        for j in range(jobs):
-            @pl.when(t == 2 * j)
+        for j in range(1, jobs):
+            @pl.when(t == 4 * j)
             def _():
-                stay(j).wait()
                 pair(j).wait()
                 onward(j).wait()
 
         @pl.when(t < units)
         def _():
-            job = t // 2
-            which = jnp.where(t == 2 * (jobs - 1), 2, lax.rem(t, 2))
-            for c in range(width // 256):
-                lanes = slice(c * 256, c * 256 + 256)
-                part[t, :, lanes] = jnp.dot(
+            job = t // 4
+            which = jnp.where(t >= 4 * (jobs - 1), 2, lax.rem(t // 2, 2))
+            column = lax.rem(t, 2) * narrow
+            for c in range(narrow // 256):
+                lanes = pl.ds(pl.multiple_of(column + c * 256, 256), 256)
+                part[t, :, c * 256 : c * 256 + 256] = jnp.dot(
                     x_ref[which], blocks[job, :, lanes], preferred_element_type=jnp.float32
                 ).astype(part.dtype)
 
@@ -476,7 +615,7 @@
                     @pl.when(ctx > 0)
                     def _():
                         going_up(u, k).wait_recv()
-                        add(u, k, below)
+                        add(u, k)
 
                     going_up(u, k).start()
 
@@ -489,10 +628,41 @@
                 def _():
                     @pl.when(ctx < last)
                     def _():
-                        going_down(v, k).wait_recv()
-                        add(v, k, above)
+                        coming_down(v, k).wait_recv()
+                        add(v, k)
 
                     going_down(v, k).start()
+
+        @pl.when(t < steps)
+        def _():
+            slot = lax.rem(t, 2)
+
+            @pl.when(t + 1 < steps)
+            def _():
+                for copy in load(t + 1, 1 - slot):
+                    copy.start()
+
+            for copy in load(t, slot):
+                copy.wait()
+            mine = rows_of(shard)
+            left = (blocks[1, mine, :], blocks[2, mine, :], gate_s[...], blocks[0, mine, :])
+            total = None
+            for k, rows in enumerate(left):
+                weight = weight_s[slot, k // 2, :, :, (k % 2) * width : (k % 2) * width + width]
+                term = lax.dot_general(rows, weight.reshape(2 * features, width), (((1,), (1,)), ((), ())),
+                                       preferred_element_type=jnp.float32)
+                total = term if total is None else total + term
+            total = mask_ref[:, 0:1] * total[:, :features] + mask_ref[:, 1:2] * total[:, features:]
+            at = feature_rows(t)
+            normed_ref[:, pl.ds(at, features)] = total
+
+            @pl.when(t < steps // 2)
+            def _():
+                give_s[:, pl.ds(pl.multiple_of(t * features, features), features)] = total.astype(give_s.dtype)
+
+            @pl.when(t == steps // 2)
+            def _():
+                beside_copy().start()
 
         w = t - last
 
@@ -504,21 +674,22 @@
             @pl.when(ctx > 0)
             def _():
                 going_up(w, ctx).wait_recv()
-                sum_ref[w] += below[w, rows, :].astype(jnp.float32)
+                sum_ref[w] += came[w, rows, :].astype(jnp.float32)
 
             @pl.when(ctx < last)
             def _():
-                going_down(w, ctx).wait_recv()
-                sum_ref[w] += above[w, rows, :].astype(jnp.float32)
+                coming_down(w, ctx).wait_recv()
+                sum_ref[w] += came[w, (last + 1) * deep :, :].astype(jnp.float32)
 
         for j in range(1, jobs):
-            @pl.when(t == 2 * j - 1)
+            @pl.when(t == 4 * j - 2)
             def _():
                 advance(j)
 
         return 0
 
     lax.fori_loop(0, units + last, step, 0)
+    beside_copy().wait()
 
     def drain(u, _):
         for k in range(last + 1):
@@ -535,28 +706,71 @@
     lax.fori_loop(0, units, drain, 0)
 
 
-def finish_weights(x, g_gate, g_conv_in, gated):
+def finish_weights(x, first, g_conv_in, gated, g_gate, masks, conv_weight, gate_weight):
     _, features, group = x.shape
-    tokens, width = g_gate.shape
-    jobs, units = 4, 7
+    tokens, width = gated.shape
+    jobs, units, narrow = 4, 14, width // 2
     deep = features // 4
+    total = conv_weight.shape[1]
     any_space = pl.BlockSpec(memory_space=pl.ANY)
     vmem = pl.BlockSpec(memory_space=pltpu.VMEM)
     sums = pltpu.SemaphoreType.DMA((units, 4))
     job_sems = pltpu.SemaphoreType.DMA((jobs,))
-    flops = 2 * units * features * group * width
+    two = pltpu.SemaphoreType.DMA((2,))
+    flops = 2 * units * features * group * narrow + 8 * tokens * total * 2 * width * 2
     return pl.pallas_call(
         finish_kernel,
-        in_specs=[vmem, any_space, any_space, any_space],
-        out_specs=vmem,
-        out_shape=jax.ShapeDtypeStruct((units, deep, width), jnp.float32),
-        scratch_shapes=[pltpu.VMEM((jobs, group, width), jnp.bfloat16)]
-        + [pltpu.VMEM((units, features, width), jnp.bfloat16)] * 3
-        + [job_sems] * 7 + [sums] * 4,
+        in_specs=[vmem] + [any_space] * 7 + [vmem] + [any_space] * 2,
+        out_specs=[vmem] * 3,
+        out_shape=[jax.ShapeDtypeStruct((units, deep, narrow), jnp.float32),
+                   jax.ShapeDtypeStruct((tokens, total), jnp.float32),
+                   jax.ShapeDtypeStruct((tokens, total // 2), jnp.bfloat16)],
+        scratch_shapes=[pltpu.VMEM((jobs, group, width), jnp.bfloat16),
+                        pltpu.VMEM((units, features, narrow), jnp.bfloat16),
+                        pltpu.VMEM((units, 5 * deep, narrow), jnp.bfloat16),
+                        pltpu.VMEM((tokens, width), jnp.bfloat16),
+                        pltpu.VMEM((2, 2, 2, 128, 2 * width), jnp.bfloat16),
+                        pltpu.VMEM((tokens, total // 2), jnp.bfloat16)]
+        + [job_sems] * 8 + [two, pltpu.SemaphoreType.DMA((2, 2)), two] + [sums] * 4,
         compiler_params=pltpu.CompilerParams(collective_id=2, has_side_effects=True, vmem_limit_bytes=VMEM_LIMIT),
         cost_estimate=pl.CostEstimate(flops=flops, bytes_accessed=500_000_000, transcendentals=0),
         name="finish_weights",
-    )(x, g_gate, g_conv_in, gated)
+    )(x, *first, g_conv_in, gated, g_gate, masks, conv_weight, gate_weight)
+
+
+def scan_entering(raw, conv, gate, gg, a2, b, c, cut, normed, g_mix, flags, seqs):
+    blocks, states, groups, _ = a2.shape
+    rows = raw.shape[0]
+    tokens = rows // seqs
+    width = groups * 128
+    steps = blocks * seqs
+    smem = pl.BlockSpec(memory_space=pltpu.SMEM)
+    any_space = pl.BlockSpec(memory_space=pl.ANY)
+    vmem = pl.BlockSpec(memory_space=pltpu.VMEM)
+    token = pl.BlockSpec((tokens, width), lambda j, s: (s, j))
+    elements = raw.size * states
+    ends = pltpu.VMEM((steps, 2, states * groups, 128), jnp.bfloat16)
+    came = pltpu.VMEM((3, steps, 2, states * groups, 128), jnp.bfloat16)
+    sums = pltpu.SemaphoreType.DMA((steps, 3))
+    nine = pltpu.SemaphoreType.DMA((3, 3))
+    state = jax.ShapeDtypeStruct((steps, states * groups, 128), jnp.float32)
+    group = jax.ShapeDtypeStruct((4 * rows, normed.shape[1] // 4), jnp.bfloat16)
+    h0, q0, *lists = pl.pallas_call(
+        functools.partial(entering_kernel, groups, states, seqs),
+        grid=(blocks, seqs),
+        in_specs=[token] * 4
+        + [pl.BlockSpec((None, states, groups, 128), lambda j, s: (j, 0, 0, 0)), smem, smem, smem]
+        + [any_space] * 3,
+        out_specs=[vmem] * 2 + [any_space] * 3,
+        out_shape=[state, state, group, group, jax.ShapeDtypeStruct((flags.shape[0], 4 * rows), jnp.bfloat16)],
+        scratch_shapes=[pltpu.VMEM((tokens * groups, 128), jnp.float32)] * 3 + [ends] * 2 + [came] * 2
+        + [sums] * 4 + [nine] * 2 + [pltpu.SemaphoreType.DMA((3,))],
+        compiler_params=pltpu.CompilerParams(collective_id=4, has_side_effects=True, vmem_limit_bytes=VMEM_LIMIT),
+        cost_estimate=pl.CostEstimate(flops=8 * elements, bytes_accessed=elements, transcendentals=elements),
+        name="scan_entering",
+    )(raw, conv, gate, gg, a2, b.reshape(-1), c.reshape(-1), cut.reshape(-1), normed, g_mix, flags)
+    shape = (blocks, seqs, states, groups, 128)
+    return h0.reshape(shape), q0.reshape(shape), lists
 
 
 def small_kernel(in_ref, out_ref, x_in, mine, y_in, z_in, x_sem, a_send, a_recv, b_send, b_recv, c_send, c_recv):
@@ -659,30 +873,10 @@
     return state, adjoint
 
 
-def group_rows(normed, g_mix, masks, fast):
-    modes, tokens = masks.shape
-    count = lax.axis_size("shard")
-    width = normed.shape[1]
-    deep = width // count
-    if not fast:
-        both = lax.all_to_all(jnp.stack([normed, g_mix]), "shard", 2, 1, tiled=True)
-        flags = lax.all_gather(masks, "shard", axis=1, tiled=True)
-        return jnp.stack([(both[0] * flags[index][:, None]).T for index in range(modes)] + [both[1].T])
-    flags = jnp.broadcast_to(jnp.pad(masks, ((0, 16 - modes), (0, 0))), (count, 16, tokens))
-    bundle = jnp.concatenate(
-        [normed.T.reshape(count, deep, tokens), g_mix.T.reshape(count, deep, tokens), flags], axis=1
-    )
-    here = lax.axis_index("shard")
-    whole = jnp.zeros((2 * deep + 16, count * tokens), BF16)
-    for k in range(count):
-        piece = lax.dynamic_index_in_dim(bundle, here ^ k, 0, keepdims=False)
-        if k:
-            piece = lax.ppermute(piece, "shard", [(i, i ^ k) for i in range(count)])
-        whole = lax.dynamic_update_slice(whole, piece, (0, (here ^ k) * tokens))
-    flags = whole[2 * deep :]
-    return jnp.stack(
-        [whole[:deep] * flags[index : index + 1] for index in range(modes)] + [whole[deep : 2 * deep]]
-    )
+def group_rows(normed, g_mix, masks):
+    both = lax.all_to_all(jnp.stack([normed, g_mix]), "shard", 2, 1, tiled=True)
+    flags = lax.all_gather(masks, "shard", axis=1, tiled=True)
+    return jnp.stack([(both[0] * flag[:, None]).T for flag in flags] + [both[1].T])
 
 
 def per_device(
@@ -731,6 +925,19 @@
             total = total + product(values * masks[index], weights[index], 1, weight_dim)
         return total
 
+    def pair_total(value):
+        if tps != 2:
+            return lax.psum(value, "tp")
+        return value + lax.ppermute(value, "tp", [(0, 1), (1, 0)])
+
+    def half_total(sent, value):
+        if tps != 2:
+            return lax.psum_scatter(sent, "tp", scatter_dimension=1, tiled=True).astype(jnp.float32)
+        own = lax.axis_index("tp") * part_width
+        gift = lax.dynamic_slice_in_dim(sent, part_width - own, part_width, 1)
+        gift = lax.ppermute(gift, "tp", [(0, 1), (1, 0)])
+        return lax.dynamic_slice_in_dim(value, own, part_width, 1) + gift.astype(jnp.float32)
+
     def modal_terms(values, grads):
         return jnp.stack([product(values * masks[index], grads, 0, 0) for index in range(modes)])
 
@@ -744,7 +951,6 @@
     conv_in = product(normed_modes, conv_weight.reshape(modes * width, inner), 1, 0)
     conv_in = conv_in.astype(BF16).reshape(seqs, local_len, inner)
     gate_in = product(normed_modes, gate_weight.reshape(modes * width, inner), 1, 0)
-    x = group_rows(normed, g_mix, masks[:, :, 0], fast)
 
     def terms_of(lefts, grads):
         return jnp.stack([product(left, grads, 1, 0) for left in lefts]).astype(BF16)
@@ -768,7 +974,7 @@
         pre = pre + filter_weight[reach - lag] * taps[lag] * same[lag]
     cut = (1.0 - same[1][:, :, 0]) * 1e30
     conv_out = jax.nn.silu(pre).astype(BF16).reshape(rows, inner)
-    selected = lax.psum(apply_modes(conv_out, full_select, 1), "tp")
+    selected = pair_total(apply_modes(conv_out, full_select, 1))
     delta_low = selected[:, :rank].astype(BF16)
     b_in = selected[:, rank : rank + states]
     c_out = selected[:, rank + states :]
@@ -778,9 +984,20 @@
     neg_decay = -jnp.exp(decay_log)
     _, blocks, groups = sizes(raw, seqs, states)
     a2 = state_form(neg_decay * LOG2E, blocks, groups)
-    ends = [scan_ends(raw, conv_out, gate_in, g_gated, a2[j], b_in, c_out, cut, seqs, j) for j in range(blocks)]
-    entering = [exchange_ends(*part, "ctx") for part in ends]
-    entering[0], ends[-1], x = lax.optimization_barrier((entering[0], ends[-1], x))
+    if fast:
+        flags = jnp.pad(masks[:, :, 0], ((0, 16 - modes), (0, 0)))
+        carried, adjoint, (normed_group, g_mix_group, flags) = scan_entering(
+            raw, conv_out, gate_in, g_gated, a2, b_in, c_out, cut, normed, g_mix, flags, seqs
+        )
+        entering = list(zip(carried, adjoint))
+        normed_turned = normed_group.T
+        x = jnp.stack([normed_turned * flags[index : index + 1] for index in range(modes)] + [g_mix_group.T])
+    else:
+        entering = [
+            exchange_ends(*scan_ends(raw, conv_out, gate_in, g_gated, a2[j], b_in, c_out, cut, seqs, j), "ctx")
+            for j in range(blocks)
+        ]
+        x = group_rows(normed, g_mix, masks[:, :, 0])
     results = [
         scan_both(raw, conv_out, gate_in, g_gated, skip_gain, a2[j], *entering[j], b_in, c_out, cut, seqs, j)
         for j in range(blocks)
@@ -790,6 +1007,10 @@
         gate_all = lax.all_gather(part[1], "shard", axis=0, tiled=True)
         gated_all = lax.all_gather(part[0], "shard", axis=0, tiled=True)
         early.append((terms_of(x[:modes], gate_all), terms_of(x[modes:], gated_all)))
+    if fast:
+        first = [results[1][1]] + [
+            lax.ppermute(results[1][1], "shard", [(i, i ^ k) for i in range(4)]) for k in range(1, 4)
+        ]
     early, results = lax.optimization_barrier((early, results))
     gate_grads = [summed(part[0]) for part in early]
     out_grads = [summed(part[1])[0] for part in early]
@@ -798,12 +1019,8 @@
     g_skip = jnp.concatenate(g_skip, axis=2)
     g_neg = jnp.stack([jnp.sum(part, axis=0) for part in g_neg])
 
-    mix_local = (
-        lax.psum_scatter(
-            product(gated, full_out, 1, 0).astype(BF16), "tp", scatter_dimension=1, tiled=True
-        ).astype(jnp.float32)
-        * valid_rows
-    )
+    mix_part = product(gated, full_out, 1, 0)
+    mix_local = half_total(mix_part.astype(BF16), mix_part) * valid_rows
     local_stream = stream.reshape(rows, part_width).astype(jnp.float32)
     output = (local_stream + mix_local).astype(BF16).reshape(seqs, local_len, part_width)
     stream_sq = jnp.sum(valid_rows * jnp.sum(whole * whole, axis=1, keepdims=True))
@@ -814,7 +1031,7 @@
     delta_terms = modal_terms(delta_low, g_raw)
     g_low = apply_modes(g_raw, full_delta, 1)
     select_part = jnp.concatenate([g_low, pair_sum(sum(g_b), states), pair_sum(sum(g_c), states)], axis=1)
-    g_sel_low = lax.psum(select_part, "tp").astype(BF16)
+    g_sel_low = pair_total(select_part).astype(BF16)
     select_terms = modal_terms(g_sel_low, conv_out)
     g_conv = g_conv + apply_modes(g_sel_low, full_select, 0)
     sig_pre = jax.nn.sigmoid(pre)
@@ -831,12 +1048,20 @@
     g_conv_in = g_ext[:, reach:] + jnp.pad(returned, ((0, 0), (local_len - reach, 0), (0, 0)))
     g_conv_in = g_conv_in.reshape(rows, inner).astype(BF16)
     if fast:
-        final = finish_weights(x, results[1][1], g_conv_in, results[1][0])
-        gate_grads.append(final[0:2])
-        conv_grad = jnp.concatenate([final[2:4], final[4:6]], axis=2)
-        out_grads.append(final[6])
+        final, g_normed_part, other = finish_weights(
+            x, first, g_conv_in, results[1][0], results[0][1], masks_float[:, :, 0].T, conv_weight, gate_weight
+        )
+        halves = [jnp.concatenate([final[i], final[i + 1]], axis=1) for i in range(0, 14, 2)]
+        gate_grads.append(jnp.stack(halves[:2]))
+        conv_grad = jnp.stack([jnp.concatenate([halves[2 + m], halves[4 + m]], axis=1) for m in range(2)])
+        out_grads.append(halves[6])
     else:
         conv_grad = summed(terms_of(x[:modes], lax.all_gather(g_conv_in, "shard", axis=0, tiled=True)))
+        g_normed_part = sum(
+            product(grad * masks[index], weight[index], 1, 1)
+            for weight, grad in ((conv_weight, g_conv_in), (gate_weight, g_gate))
+            for index in range(modes)
+        )
     in_grad = jnp.stack([conv_grad, jnp.concatenate(gate_grads, axis=2)], axis=2)
     out_grad = jnp.concatenate(out_grads, axis=1).T
     group = lax.axis_size("shard") * lax.axis_size("ctx")
@@ -852,12 +1077,7 @@
     terms = terms[: modes * each].reshape(modes, each, inner)
     delta_grad, select_grad = terms[:, :deep], terms[:, deep:]
 
-    g_normed_part = sum(
-        product(grad * masks[index], weight[index], 1, 1)
-        for weight, grad in ((conv_weight, g_conv_in), (gate_weight, g_gate))
-        for index in range(modes)
-    )
-    row_total = lax.psum(jnp.sum(g_normed_part * norm_gain * whole, axis=1, keepdims=True), "tp")
+    row_total = pair_total(jnp.sum(g_normed_part * norm_gain * whole, axis=1, keepdims=True))
     gain_part = jnp.sum(g_normed_part * whole * inverse, axis=0)
     scalars = jnp.stack([stream_sq * (1.0 / tps), jnp.sum(mix_local * mix_local), count * (1.0 / tps)])
     small = jnp.concatenate([bias_grad, decay_grad, skip_grad[None], filter_grad, offset_grad[None]], axis=0)
@@ -869,10 +1089,13 @@
         small_total = lax.psum(small, ("shard", "ctx"))
         wide = lax.psum(jnp.concatenate([gain_part, scalars]), ("shard", "ctx", "tp"))
         gain_total, scalars = wide[:width], wide[width:]
-    g_normed = lax.psum_scatter(
-        g_normed_part.astype(BF16), "tp", scatter_dimension=1, tiled=True
-    ).astype(jnp.float32)
     start = lax.axis_index("tp") * part_width
+    if fast:
+        g_normed = lax.dynamic_slice_in_dim(g_normed_part, start, part_width, 1) + other.astype(jnp.float32)
+    else:
+        g_normed = lax.psum_scatter(
+            g_normed_part.astype(BF16), "tp", scatter_dimension=1, tiled=True
+        ).astype(jnp.float32)
     own_gain = lax.dynamic_slice_in_dim(norm_gain, start, part_width, 0)
     g_stream = inverse * own_gain * g_normed - local_stream * inverse**3 * row_total / width
     gain_grad = lax.dynamic_slice_in_dim(gain_total, start, part_width, 0)

time: 854 us -> 755 us (0.88)
  matrix products: 120 us -> 75.7 us
  starting transfers between devices: 29.9 us -> 11.9 us
  waiting for transfers between devices: 24 us -> 7.81 us
  blocking collectives: 14.8 us -> 0 us
    dot_general x24 -> x20, matrix products: 120 us -> 75.7 us  [product(): lax.dot_general(left, right, (((left_dim,), (right_dim,)), ((), ())), pre...]
    ppermute x14 -> x2, starting transfers between devices: 26.1 us -> 3.82 us  [from_behind(): return lax.ppermute(value, axis, pairs)]
    ppermute x14 -> x2, waiting for transfers between devices: 16.4 us -> 0.01 us  [from_behind(): return lax.ppermute(value, axis, pairs)]
    pallas_call x3 -> x2, Pallas kernels: 227 us -> 212 us  [the longest x1 158 us: finish_weights(): pl.pallas_call(finish_kernel, in_specs=[vmem] + [any_space] * 7 + [vmem]...]
    psum x2 -> x0, blocking collectives: 14.8 us -> none  [the longest x1 10.6 us: per_device(): g_sel_low = lax.psum(select_part, 'tp').astype(BF16)]
    unnamed x168 -> x167, local copies, waits for them, and re-layouts: 36.3 us -> 41.6 us
  transfers between devices with their start and end apart: 29 -> 18, of which waited for: 10 -> 1; matrix products, arithmetic and copies ran while one was open for 27% -> 25% of each run, Pallas kernels for 52% -> 51%
where the time goes in v2:
time: 755 us; the launch traced here: 746 us
  Pallas kernels  483 us (64%)
  local copies, waits for them, and re-layouts  77.9 us (10%)
  matrix products  75.7 us (10%)
  other arithmetic  68.7 us (9%)
  between operations  21.2 us (3%)
  starting transfers between devices  11.9 us (2%)
  waiting for transfers between devices  7.81 us (1%)
    pallas_call x1, Pallas kernels, finish_weights(): pl.pallas_call(finish_kernel, in_specs=[vmem] + [any_space] * 7 + [vmem]...  158 us
    pallas_call x1, Pallas kernels, gather_weights(): pl.pallas_call(functools.partial(gather_kernel, chunks), in_specs=[vmem]...  149 us
    pallas_call x2, Pallas kernels, scan_both(): pl.pallas_call(functools.partial(scan_kernel, groups, states, states, sta...  100 us
    dot_general x20, matrix products, product(): lax.dot_general(left, right, (((left_dim,), (right_dim,)), ((), ())), pre...  75.7 us
    pallas_call x1, Pallas kernels, scan_entering(): pl.pallas_call(functools.partial(entering_kernel, groups, states, seqs),...  53.4 us
    unnamed x167, local copies, waits for them, and re-layouts  41.6 us
    pallas_call x1, Pallas kernels, small_sum(): pl.pallas_call(small_kernel, in_specs=[vmem], out_specs=vmem, out_shape=j...  21.5 us
  transfers between devices with their start and end apart: 18, of which 1 were waited for; matrix products, arithmetic and copies ran while one was open for 25% of the time, Pallas kernels for 51%

profile of v2, /device:TPU:1, one launch (start us, length us, event | category | flops | bytes accessed | tf_op | source)
XLA Modules:
  0.0 745.8 jit_solution(5808178562327635927)
XLA Ops:
  10.8 10.8 %copy.111 = bf16[2,512,2,2048]{3,1,0,2:T(8,128)(2,1)} copy(bf16[2,512,2,2048]{3,2,1,0:T(2,128)(2,1)} %param.17) | data formatting | bytes 16777216 | tf_op args[2]
  21.7 6.3 slice_bitcast_fusion
  34.8 149.2 %gather_weights.1 = (bf16[2,2048,2048]{2,1,0:T(8,128)(2,1)}, bf16[2,2048,2048]{2,1,0:T(8,128)(2,1)}, bf16[2048,2048]{1,0:T(8,128)(2,1)S(1)}) custom-call(bf16[2,512,2048]{2,1,0:T(8,128)(2,1)S(1)} %copy-done.1, bf16[2,512,2048]{2,1,0:T(8,128)(2,1)S(1)} %copy-done, bf16[2048,512]{1,0:T(8,128)(2,1)S(1)} %copy-done.2), custom_call_target="tpu_custom_call" | custom-call | bytes 400000000 | tf_op jit(solution)/shard_map/gather_weights/pallas_call | solution.py:471
  184.0 3.2 copy-done.3
  193.8 12.6 %convolution_convert_fusion = bf16[512,2048]{1,0:T(8,128)(2,1)S(1)} fusion(bf16[4096,2048]{1,0:T(8,128)(2,1)} %bitcast.308, bf16[512,2048]{1,0:T(8,128)(2,1)S(1)} %broadcast_multiply_fusion.3, bf16[512,2048]{1,0:T(8,128)(2,1)S(1)} %get-tuple-element.181), kind=kOutput, calls=%fused_computation.32 | convolution fusion | flops 8599371776 | bytes 23068672 | tf_op jit(solution)/shard_map/dot_general | solution.py:857
  208.9 13.9 %fusion.7.gate_ref = f32[512,2048]{1,0:T(8,128)} fusion(bf16[4096,2048]{1,0:T(8,128)(2,1)} %bitcast.309, bf16[512,2048]{1,0:T(8,128)(2,1)S(1)} %broadcast_multiply_fusion.3, bf16[512,2048]{1,0:T(8,128)(2,1)S(1)} %get-tuple-element.181), kind=kOutput, calls=%fused_computation.33 | convolution fusion | flops 8598323200 | bytes 25165824 | tf_op jit(solution)/shard_map/dot_general | solution.py:857
  226.8 5.6 broadcast_multiply_fusion.1
  240.7 9.5 %fusion.84.gg_ref = f32[512,2048]{1,0:T(8,128)} fusion(bf16[512,2048]{1,0:T(8,128)(2,1)S(1)} %copy-done.24, bf16[2048,2048]{1,0:T(8,128)(2,1)} %copy-done.3), kind=kOutput, calls=%fused_computation.200 | convolution fusion | flops 4294967296 | bytes 14680064 | tf_op jit(solution)/shard_map/dot_general | solution.py:857
  257.0 53.4 %scan_entering.1 = (f32[4,128,128]{2,1,0:T(8,128)}, f32[4,128,128]{2,1,0:T(8,128)}, bf16[2048,512]{1,0:T(8,128)(2,1)}, bf16[2048,512]{1,0:T(8,128)(2,1)}, bf16[16,2048]{1,0:T(8,128)(2,1)}) custom-call(f32[512,2048]{1,0:T(8,128)} %add_add_fusion.raw_ref, bf16[512,2048]{1,0:T(8,128)(2,1)} %bitcast.238, f32[512,2048]{1,0:T(8,128)} %fusion.7.gate_ref, ...), custom_call_target="tpu_custom_call" | custom-call | flops 134217728 | bytes 16777216 | tf_op jit(solution)/shard_map/scan_entering/pallas_call | solution.py:758
  313.7 49.9 %scan_both.2 = (bf16[512,1024]{1,0:T(8,128)(2,1)}, bf16[512,1024]{1,0:T(8,128)(2,1)}, bf16[512,1024]{1,0:T(8,128)(2,1)}, f32[512,1024]{1,0:T(8,128)}, f32[2,16,8...) custom-call(f32[512,2048]{1,0:T(8,128)} %add_add_fusion.raw_ref, ...), custom_call_target="tpu_custom_call" | custom-call | flops 184549376 | bytes 16777216 | tf_op jit(solution)/shard_map/scan_both/pallas_call | solution.py:363
  367.1 50.2 %scan_both.3 = (bf16[512,1024]{1,0:T(8,128)(2,1)}, bf16[512,1024]{1,0:T(8,128)(2,1)}, bf16[512,1024]{1,0:T(8,128)(2,1)}, f32[512,1024]{1,0:T(8,128)}, f32[2,16,8...) custom-call(f32[512,2048]{1,0:T(8,128)} %add_add_fusion.raw_ref, ...), custom_call_target="tpu_custom_call" | custom-call | flops 184549376 | bytes 16777216 | tf_op jit(solution)/shard_map/scan_both/pallas_call | solution.py:363
  422.4 3.9 copy.83
  431.1 4.7 fusion.40
  439.7 4.6 all-gather.17.cloned.1.call-done
  444.3 5.5 fusion.36
  461.8 7.4 fusion.18
  486.7 4.2 multiply_reduce_fusion
  501.0 10.6 %pad_add_fusion = f32[2,259,2048]{2,1,0:T(8,128)} fusion(f32[2,256,2048]{2,1,0:T(8,128)} %copy-done.6, f32[2,256,2048]{2,1,0:T(8,128)} %copy-done.7, f32[2,256,2048]{2,1,0:T(8,128)} %copy-done.8, f32[2,256,2048]{2,1,0:T(8,128)} %copy-done.5), kind=kLoop, calls=%fused_computation.2 | loop fusion | flops 3182592 | bytes 21020672 | tf_op jit(solution)/shard_map/add | solution.py:1045
  516.0 4.1 fusion
  520.1 158.4 %finish_weights.1 = (f32[14,128,512]{2,1,0:T(8,128)}, f32[512,2048]{1,0:T(8,128)}, bf16[512,1024]{1,0:T(8,128)(2,1)}) custom-call(bf16[3,512,2048]{2,1,0:T(8,128)(2,1)} %pad_maximum_fusion.x_ref, bf16[512,1024]{1,0:T(8,128)(2,1)} %get-tuple-element.75.first_0, bf16[512,1024]{1,0:T(8,128)(2,1)} %collective-permute-done.3.first_1, ...), custom_call_target="tpu_custom_call" | custom-call | flops 49392123904 | bytes 500000000 | tf_op jit(solution)/shard_map/finish_weights/pallas_call | solution.py:721
  678.5 3.6 fusion.6
  689.7 4.4 multiply_reduce_fusion.4
  695.2 21.5 %small_sum.1 = f32[32,2048]{1,0:T(8,128)S(1)} custom-call(f32[32,2048]{1,0:T(8,128)S(1)} %concatenate.72.in_ref), custom_call_target="tpu_custom_call" | custom-call | bytes 40000000 | tf_op jit(solution)/shard_map/small_sum/pallas_call | solution.py:830
  728.9 5.3 copy.92
  (318 shorter events, 121.7 us)
Async XLA Ops:
  7.2 180.1 %all-gather.7.cloned.1.call-start = ((), (), s32[]{:S(2)}) async-start(), calls=%async_computation.3 | async-start | bytes 3145728 | tf_op jit(solution)/shard_map/all_gather | solution.py:947
  7.9 215.0 %all-gather.13.cloned.1.call-start = ((), (), s32[]{:S(2)}) async-start(), calls=%async_computation.6 | async-start | bytes 3145728 | tf_op jit(solution)/shard_map/all_gather | solution.py:944
  8.7 225.5 %all-gather.9.cloned.1.call-start = ((), (), s32[]{:S(2)}) async-start(), calls=%async_computation.4 | async-start | bytes 1638400 | tf_op jit(solution)/shard_map/all_gather | solution.py:914
  9.4 242.6 %all-gather.11.cloned.1.call-start = ((), (), s32[]{:S(2)}) async-start(), calls=%async_computation.5 | async-start | bytes 1310720 | tf_op jit(solution)/shard_map/all_gather | solution.py:915
  10.0 421.2 %all-gather.15.cloned.1.call-start = ((), (), s32[]{:S(2)}) async-start(), calls=%async_computation.7 | async-start | bytes 5242880 | tf_op jit(solution)/shard_map/all_gather | solution.py:1007
  10.8 243.1 %copy-start.54 = (bf16[1,2,2,128]{3,1,2,0:T(2,128)(2,1)}, bf16[1,2,2,128]{3,1,2,0:T(2,128)(2,1)S(1)}, u32[]{:S(2)}) copy-start(bf16[1,2,2,128]{3,1,2,0:T(2,128)(2,1)S(1)} %copy.96) | copy-start | bytes 3076
  10.8 241.2 %copy-start.51 = (bf16[1,2,2,128]{3,1,2,0:T(2,128)(2,1)}, bf16[1,2,2,128]{3,1,2,0:T(2,128)(2,1)S(1)}, u32[]{:S(2)}) copy-start(bf16[1,2,2,128]{3,1,2,0:T(2,128)(2,1)S(1)} %copy.97) | copy-start | bytes 3076
  28.1 198.6 %copy-start.60 = (f32[2,256]{1,0:T(2,128)}, f32[2,256]{1,0:T(2,128)S(1)}, u32[]{:S(2)}) copy-start(f32[2,256]{1,0:T(2,128)S(1)} %get-tuple-element.228) | copy-start | bytes 6148
  28.1 198.6 %copy-start.62 = (f32[2,256]{1,0:T(2,128)}, f32[2,256]{1,0:T(2,128)S(1)}, u32[]{:S(2)}) copy-start(f32[2,256]{1,0:T(2,128)S(1)} %get-tuple-element.229) | copy-start | bytes 6148
  28.2 198.5 %copy-start.64 = (f32[2,256]{1,0:T(2,128)}, f32[2,256]{1,0:T(2,128)S(1)}, u32[]{:S(2)}) copy-start(f32[2,256]{1,0:T(2,128)S(1)} %get-tuple-element.177) | copy-start | bytes 6148
  28.3 198.5 %copy-start.42 = (f32[1,2048]{1,0:T(1,128)}, f32[1,2048]{1,0:T(1,128)S(1)}, u32[]{:S(2)}) copy-start(f32[1,2048]{1,0:T(1,128)S(1)} %get-tuple-element.224) | copy-start | bytes 24580
  206.4 19.7 %collective-permute-start = (bf16[2,3,2048]{2,1,0:T(4,128)(2,1)S(1)}, bf16[2,3,2048]{2,1,0:T(4,128)(2,1)S(1)}, u32[]{:S(2)}, u32[]{:S(2)}) collective-permute-start(bf16[2,3,2048]{2,1,0:T(4,128)(2,1)S(1)} %slice.266), channel_id=1, source_target_pairs={{0,2},{2,4},{4,6},{1,3},{3,5},{5,7},{8,10},{10,12},{12,14},{9,11},... | collective-permute-start | bytes 73736 | tf_op jit(solution)/shard_map/ppermute | solution.py:853
  239.4 10.8 %collective-permute-start.1 = (f32[512,160]{0,1:T(8,128)S(1)}, f32[512,160]{0,1:T(8,128)S(1)}, u32[]{:S(2)}, u32[]{:S(2)}) collective-permute-start(f32[512,160]{0,1:T(8,128)S(1)} %convolution_add_fusion), channel_id=1, source_target_pairs={{0,1},{1,0},{2,3},{3,2},{4,5},{5,4},{6,7},{7,6},{8,9},{9,8},{10,11... | collective-permute-start | bytes 983048 | tf_op jit(solution)/shard_map/ppermute | solution.py:931
  363.7 80.6 %all-gather.17.cloned.1.call-start = ((), (), s32[]{:S(2)}) async-start(), calls=%async_computation.8 | async-start | bytes 5242880 | tf_op jit(solution)/shard_map/all_gather | solution.py:1008
  364.3 358.2 %reduce-scatter.8.cloned.1.call-start = ((), (), s32[]{:S(2)}) async-start(), calls=%async_computation.11 | async-start | bytes 1310720 | tf_op jit(solution)/shard_map/reduce_scatter | solution.py:959
  417.3 102.8 %collective-permute-start.3 = (bf16[512,1024]{1,0:T(8,128)(2,1)}, bf16[512,1024]{1,0:T(8,128)(2,1)}, u32[]{:S(2)}, u32[]{:S(2)}) collective-permute-start(bf16[512,1024]{1,0:T(8,128)(2,1)} %get-tuple-element.75.first_0), channel_id=1, source_target_pairs={{0,8},{8,0},{16,24},{24,16},{1,9},{9,1},{17,25},{25,17},{2,10},{10... | collective-permute-start | bytes 3145736 | tf_op jit(solution)/shard_map/ppermute | solution.py:1012
  417.4 102.7 %collective-permute-start.4 = (bf16[512,1024]{1,0:T(8,128)(2,1)}, bf16[512,1024]{1,0:T(8,128)(2,1)}, u32[]{:S(2)}, u32[]{:S(2)}) collective-permute-start(bf16[512,1024]{1,0:T(8,128)(2,1)} %get-tuple-element.75.first_0), channel_id=1, source_target_pairs={{0,16},{8,24},{16,0},{24,8},{1,17},{9,25},{17,1},{25,9},{2,18},{10... | collective-permute-start | bytes 3145736 | tf_op jit(solution)/shard_map/ppermute | solution.py:1012
  418.5 101.6 %collective-permute-start.5 = (bf16[512,1024]{1,0:T(8,128)(2,1)}, bf16[512,1024]{1,0:T(8,128)(2,1)}, u32[]{:S(2)}, u32[]{:S(2)}) collective-permute-start(bf16[512,1024]{1,0:T(8,128)(2,1)} %get-tuple-element.75.first_0), channel_id=1, source_target_pairs={{0,24},{8,16},{16,8},{24,0},{1,25},{9,17},{17,9},{25,1},{2,26},{10... | collective-permute-start | bytes 3145736 | tf_op jit(solution)/shard_map/ppermute | solution.py:1012
  459.2 21.6 %collective-permute-start.6 = (f32[512,160]{0,1:T(8,128)}, f32[512,160]{0,1:T(8,128)}, u32[]{:S(2)}, u32[]{:S(2)}) collective-permute-start(f32[512,160]{0,1:T(8,128)} %pad_maximum_fusion.6), channel_id=1, source_target_pairs={{0,1},{1,0},{2,3},{3,2},{4,5},{5,4},{6,7},{7,6},{8,9},{9,8},{10,11... | collective-permute-start | bytes 983048 | tf_op jit(solution)/shard_map/ppermute | solution.py:931
  461.7 264.2 %reduce-scatter.4.cloned.1.call-start = ((), (), s32[]{:S(2)}) async-start(), calls=%async_computation.9 | async-start | bytes 2621440 | tf_op jit(solution)/shard_map/reduce_scatter | solution.py:959
  472.3 215.0 %collective-permute-start.2 = (bf16[512,1024]{1,0:T(8,128)(2,1)}, bf16[512,1024]{1,0:T(8,128)(2,1)}, u32[]{:S(2)}, u32[]{:S(2)}) collective-permute-start(bf16[512,1024]{1,0:T(8,128)(2,1)} %dynamic-slice_convert_fusion), channel_id=1, source_target_pairs={{0,1},{1,0},{2,3},{3,2},{4,5},{5,4},{6,7},{7,6},{8,9},{9,8},{10,11... | collective-permute-start | bytes 3145736 | tf_op jit(solution)/shard_map/ppermute | solution.py:938
  477.4 256.7 %reduce-scatter.6.cloned.1.call-start = ((), (), s32[]{:S(2)}) async-start(), calls=%async_computation.10 | async-start | bytes 3342336 | tf_op jit(solution)/shard_map/reduce_scatter | solution.py:1073
  499.0 17.0 %collective-permute-start.7 = (f32[2,3,2048]{2,1,0:T(4,128)S(1)}, f32[2,3,2048]{2,1,0:T(4,128)S(1)}, u32[]{:S(2)}, u32[]{:S(2)}) collective-permute-start(f32[2,3,2048]{2,1,0:T(4,128)S(1)} %pad_add_fusion.1), channel_id=1, source_target_pairs={{2,0},{4,2},{6,4},{3,1},{5,3},{7,5},{10,8},{12,10},{14,12},{11,9},... | collective-permute-start | bytes 147464 | tf_op jit(solution)/shard_map/ppermute | solution.py:853
  682.2 5.1 collective-permute-start.8
  (72 other events, 1660.6 us)
Sparse Core Ops, SparseCore 0:
  9.6 35.1 all-gather.6
  46.3 33.1 all-gather.12
  81.0 25.7 all-gather.8
  108.2 22.4 all-gather.10
  363.8 33.3 all-gather.14
  398.6 45.6 all-gather.16
  461.8 26.9 reduce-scatter.7
  491.2 43.8 reduce-scatter.3
  538.9 84.1 reduce-scatter.5

commit v3 on v2

--- a/solution.py
+++ b/solution.py
@@ -6,6 +6,7 @@
 from jax.experimental.pallas import tpu as pltpu
 
 LOG2E = 1.4426950408889634
+EPSILON = 1e-05
 VMEM_LIMIT = 60 * 1024 * 1024
 
 
@@ -387,97 +388,215 @@
 MESH = pl.DeviceIdType.MESH
 
 
-def gather_kernel(chunks, conv_ref, gate_ref, out_ref, conv_full, gate_full, out_full, local_sem, core_send,
-                  core_recv, y_send, y_recv, z_send, z_recv, pass_send, pass_recv, rest_send, rest_recv):
-    shard, ctx = lax.axis_index("shard"), lax.axis_index("ctx")
-    mine, far = shard, lax.rem(shard + 2, 4)
-    core = {"shard": shard + 1 - 2 * lax.rem(shard, 2)}
-    across = {"shard": far}
+def front_kernel(in_ref, out_ref, stream_ref, gain_ref, mask_ref, conv_full, gate_full, out_full, conv_in, gate_in,
+                 normed_ref, whole_ref, conv_s, rows_s, weight_s, theirs, x_sem, load_sem, stay_sem, core_send,
+                 core_recv, y_send, y_recv, z_send, z_recv, pass_send, pass_recv, rest_send, rest_recv):
+    shard, ctx, tp = lax.axis_index("shard"), lax.axis_index("ctx"), lax.axis_index("tp")
+    near, far, beyond = shard + 1 - 2 * lax.rem(shard, 2), lax.rem(shard + 2, 4), 3 - shard
+    core, across, beside = {"shard": near}, {"shard": far}, {"tp": 1 - tp}
     side = {"ctx": ctx + 1 - 2 * lax.rem(ctx, 2)}
     half = lax.rem(ctx, 2)
-    depth = conv_ref.shape[1]
+    kinds, modes, depth, inner = in_ref.shape
     columns = out_ref.shape[1]
-    piece = depth // 2 // chunks
-    piece_out = out_ref.shape[0] // 2 // chunks
+    tokens, part_width = stream_ref.shape
+    width = 2 * part_width
+    piece, piece_out = depth // 4, out_ref.shape[0] // 4
+    inside = kinds * modes * 2
+    chunks = inside + 2
+    fulls = (conv_full, gate_full)
+    totals = (conv_s, gate_in)
 
     barrier = pltpu.get_barrier_semaphore()
-    for peer in (core, across, side):
+    for peer in (core, across, side, beside):
         pl.semaphore_signal(barrier, inc=1, device_id=peer, device_id_type=MESH)
-    pl.semaphore_wait(barrier, 3)
-
-    def views(owner, part, i):
-        rows = pl.ds(pl.multiple_of(owner * depth + (part * chunks + i) * piece, piece), piece)
-        tall = pl.ds(pl.multiple_of((part * chunks + i) * piece_out, piece_out), piece_out)
-        wide = pl.ds(pl.multiple_of(owner * columns, columns), columns)
-        return conv_full.at[:, rows], gate_full.at[:, rows], out_full.at[tall, wide]
-
-    def own(part, i):
-        rows = pl.ds(pl.multiple_of((part * chunks + i) * piece, piece), piece)
-        tall = pl.ds(pl.multiple_of((part * chunks + i) * piece_out, piece_out), piece_out)
-        return conv_ref.at[:, rows], gate_ref.at[:, rows], out_ref.at[tall, :]
-
-    def send(source, target, to, send_sem, recv_sem):
-        copies = [
-            pltpu.make_async_remote_copy(src_ref=s, dst_ref=t, send_sem=send_sem.at[k], recv_sem=recv_sem.at[k],
-                                         device_id=to, device_id_type=MESH)
-            for k, (s, t) in enumerate(zip(source, target))
-        ]
-        for copy in copies:
-            copy.start()
-        return copies
-
-    def cross(i):
-        return send(own(half, i), views(mine, half, i), across, y_send.at[i], y_recv.at[i])
-
-    to_far = [cross(i) for i in range(min(2, chunks))]
-    rows = pl.ds(pl.multiple_of(mine * depth, depth), depth)
-    wide = pl.ds(pl.multiple_of(mine * columns, columns), columns)
-    source = (conv_ref, gate_ref, out_ref)
-    place = (conv_full.at[:, rows], gate_full.at[:, rows], out_full.at[:, wide])
-    stay = [pltpu.make_async_copy(s, t, local_sem.at[k]) for k, (s, t) in enumerate(zip(source, place))]
-    for copy in stay:
-        copy.start()
-    to_core = send(source, place, core, core_send, core_recv)
-    onward = []
-    for i in range(chunks):
-        for copy in to_far[i]:
-            copy.wait()
-        if i + 2 < chunks:
-            to_far.append(cross(i + 2))
-        held = views(far, half, i)
-        onward.append(send(held, held, side, z_send.at[i], z_recv.at[i]))
-        to_core += send(held, held, core, pass_send.at[i], pass_recv.at[i])
-    for i in range(chunks):
-        for copy in onward[i]:
-            copy.wait_recv()
-        held = views(far, 1 - half, i)
-        to_core += send(held, held, core, rest_send.at[i], rest_recv.at[i])
-    for copy in stay:
-        copy.wait()
-    for copy in to_core:
-        copy.wait()
-    for i in range(chunks):
-        for copy in onward[i]:
-            copy.wait_send()
-
-
-def gather_weights(in_own, out_own, chunks=8):
-    _, modes, depth, inner = in_own.shape
+    pl.semaphore_wait(barrier, 4)
+
+    def remote(source, target, send_sem, recv_sem, to):
+        return pltpu.make_async_remote_copy(src_ref=source, dst_ref=target, send_sem=send_sem, recv_sem=recv_sem,
+                                            device_id=to, device_id_type=MESH)
+
+    def span(start, count):
+        return pl.ds(pl.multiple_of(start, count), count)
+
+    def view(owner, part, c):
+        if c < inside:
+            rows = span(owner * depth + (part * 2 + c % 2) * piece, piece)
+            return fulls[c // (2 * modes)].at[c // 2 % modes, rows]
+        return out_full.at[span((part * 2 + c - inside) * piece_out, piece_out), span(owner * columns, columns)]
+
+    def own(part, c):
+        if c < inside:
+            return in_ref.at[c // (2 * modes), c // 2 % modes, span((part * 2 + c % 2) * piece, piece)]
+        return out_ref.at[span((part * 2 + c - inside) * piece_out, piece_out), :]
+
+    def cross(c):
+        return remote(own(half, c), view(shard, half, c), y_send.at[c], y_recv.at[c], across)
+
+    def onward(c):
+        return remote(view(far, half, c), view(far, half, c), z_send.at[c], z_recv.at[c], side)
+
+    def passed(c):
+        return remote(view(far, half, c), view(far, half, c), pass_send.at[c], pass_recv.at[c], core)
+
+    def rest(c):
+        return remote(view(far, 1 - half, c), view(far, 1 - half, c), rest_send.at[c], rest_recv.at[c], core)
+
+    def place(h, m):
+        return fulls[h].at[m, span(shard * depth, depth)]
+
+    def to_core(i):
+        if i < kinds * modes:
+            h, m = i // modes, i % modes
+            return remote(in_ref.at[h, m], place(h, m), core_send.at[i], core_recv.at[i], core)
+        return remote(out_ref, out_full.at[:, span(shard * columns, columns)], core_send.at[i], core_recv.at[i], core)
+
+    def load(source, slot, count):
+        return pltpu.make_async_copy(source, weight_s.at[slot, pl.ds(0, count)], load_sem.at[slot])
+
+    def multiply(h, m, start, count, slot, fresh=False):
+        rows = rows_s[m, :, span(start, count)]
+
+        def tile(j, _):
+            lanes = span(j * 256, 256)
+            term = jnp.dot(rows, weight_s[slot, :count, lanes], preferred_element_type=jnp.float32)
+            totals[h][:, lanes] = term if fresh else totals[h][:, lanes] + term
+            return 0
+
+        lax.fori_loop(0, inner // 256, tile, 0)
+
+    def run(blocks):
+        load(blocks[0][4], 0, blocks[0][3]).start()
+        for i, (h, m, start, count, source) in enumerate(blocks):
+            if i + 1 < len(blocks):
+                load(blocks[i + 1][4], (i + 1) % 2, blocks[i + 1][3]).start()
+            load(source, i % 2, count).wait()
+            multiply(h, m, start, count, i % 2)
+
+    def own_shard():
+        for i in range(kinds * modes):
+            h, m = i // modes, i % modes
+            load(in_ref.at[h, m], i % 2, depth).start()
+            load(in_ref.at[h, m], i % 2, depth).wait()
+            stay = pltpu.make_async_copy(weight_s.at[i % 2], place(h, m), stay_sem.at[0])
+            stay.start()
+            multiply(h, m, shard * depth, depth, i % 2, fresh=m == 0)
+            stay.wait()
+
+    def near_shard():
+        for i in range(kinds * modes):
+            to_core(i).wait_recv()
+        run([(i // modes, i % modes, near * depth, depth,
+              fulls[i // modes].at[i % modes, span(near * depth, depth)]) for i in range(kinds * modes)])
+
+    def quarter(i, owner, part):
+        h, m = i // modes, i % modes
+        start = owner * depth + part * (depth // 2)
+        return h, m, start, depth // 2, fulls[h].at[m, span(start, depth // 2)]
+
+    def direct(i):
+        for c in (2 * i, 2 * i + 1):
+            passed(c).wait_recv()
+        run([quarter(i, far, half), quarter(i, beyond, half)])
+
+    def relayed(i):
+        for c in (2 * i, 2 * i + 1):
+            rest(c).wait_recv()
+        run([quarter(i, far, 1 - half), quarter(i, beyond, 1 - half)])
+
+    def normed_rows():
+        mine, other = span(tp * part_width, part_width), span((1 - tp) * part_width, part_width)
+
+        def block(i, _):
+            rows = span(i * 16, 16)
+            left = stream_ref[rows, :].astype(jnp.float32)
+            right = theirs[rows, :].astype(jnp.float32)
+            square = jnp.sum(left * left, axis=1, keepdims=True) + jnp.sum(right * right, axis=1, keepdims=True)
+            inverse = lax.rsqrt(square * (1.0 / width) + EPSILON)
+            for lanes, value in ((mine, left), (other, right)):
+                whole_ref[rows, lanes] = value.astype(whole_ref.dtype)
+                result = (value * inverse * gain_ref[:, lanes]).astype(normed_ref.dtype)
+                normed_ref[rows, lanes] = result
+                for m in range(modes):
+                    masked = result.astype(jnp.float32) * mask_ref[rows, m : m + 1]
+                    rows_s[m, rows, lanes] = masked.astype(rows_s.dtype)
+            return 0
+
+        lax.fori_loop(0, tokens // 16, block, 0)
+
+    across_tp = remote(stream_ref, theirs, x_sem.at[0], x_sem.at[1], beside)
+    across_tp.start()
+    cross(0).start()
+    cross(1).start()
+    stay_out = pltpu.make_async_copy(out_ref, out_full.at[:, span(shard * columns, columns)], stay_sem.at[1])
+    stay_out.start()
+    for i in range(kinds * modes + 1):
+        to_core(i).start()
+
+    work = {2: [own_shard], 3: [near_shard], 4: [lambda: direct(0)], 5: [lambda: relayed(0), lambda: direct(1)],
+            6: [lambda: relayed(1)], 7: [lambda: direct(2)], 8: [lambda: relayed(2)],
+            9: [lambda: direct(3), lambda: relayed(3)]}
+    for c in range(chunks):
+        cross(c).wait()
+        if c + 2 < chunks:
+            cross(c + 2).start()
+        onward(c).start()
+        passed(c).start()
+        if c:
+            onward(c - 1).wait_recv()
+            rest(c - 1).start()
+        if c == 1:
+            across_tp.wait()
+            normed_rows()
+        for task in work.get(c, []):
+            task()
+    onward(chunks - 1).wait_recv()
+    rest(chunks - 1).start()
+
+    def cast(i, _):
+        rows = span(i * 16, 16)
+        conv_in[rows, :] = conv_s[rows, :].astype(conv_in.dtype)
+        return 0
+
+    lax.fori_loop(0, tokens // 16, cast, 0)
+    stay_out.wait()
+    to_core(kinds * modes).wait_recv()
+    for i in range(kinds * modes + 1):
+        to_core(i).wait_send()
+    for c in range(chunks):
+        if c >= inside:
+            passed(c).wait_recv()
+            rest(c).wait_recv()
+        onward(c).wait_send()
+        passed(c).wait_send()
+        rest(c).wait_send()
+
+
+def front(in_own, out_own, stream, gain, masks):
+    kinds, modes, depth, inner = in_own.shape
+    tokens, part_width = stream.shape
+    width = gain.shape[0]
+    chunks = kinds * modes * 2 + 2
     any_space = pl.BlockSpec(memory_space=pl.ANY)
     vmem = pl.BlockSpec(memory_space=pltpu.VMEM)
-    many = pltpu.SemaphoreType.DMA((chunks, 3))
-    three = pltpu.SemaphoreType.DMA((3,))
+    many = pltpu.SemaphoreType.DMA((chunks,))
+    two = pltpu.SemaphoreType.DMA((2,))
+    five = pltpu.SemaphoreType.DMA((kinds * modes + 1,))
     full = jax.ShapeDtypeStruct((modes, 4 * depth, inner), in_own.dtype)
+    low = jax.ShapeDtypeStruct((tokens, width), jnp.bfloat16)
     return pl.pallas_call(
-        functools.partial(gather_kernel, chunks),
-        in_specs=[vmem] * 3,
-        out_specs=[any_space] * 3,
-        out_shape=[full, full, jax.ShapeDtypeStruct((inner, 4 * out_own.shape[1]), out_own.dtype)],
-        scratch_shapes=[three] * 3 + [many] * 8,
-        compiler_params=pltpu.CompilerParams(collective_id=1, has_side_effects=True, vmem_limit_bytes=32 * 2**20),
+        front_kernel,
+        in_specs=[any_space] + [vmem] * 4,
+        out_specs=[any_space] * 3 + [vmem] * 4,
+        out_shape=[full, full, jax.ShapeDtypeStruct((inner, 4 * out_own.shape[1]), out_own.dtype),
+                   jax.ShapeDtypeStruct((tokens, inner), jnp.bfloat16),
+                   jax.ShapeDtypeStruct((tokens, inner), jnp.float32), low, low],
+        scratch_shapes=[pltpu.VMEM((tokens, inner), jnp.float32), pltpu.VMEM((modes, tokens, width), jnp.bfloat16),
+                        pltpu.VMEM((2, depth, inner), jnp.bfloat16), pltpu.VMEM(stream.shape, jnp.bfloat16)]
+        + [two] * 3 + [five] * 2 + [many] * 8,
+        compiler_params=pltpu.CompilerParams(collective_id=1, has_side_effects=True, vmem_limit_bytes=VMEM_LIMIT),
         cost_estimate=pl.CostEstimate(flops=0, bytes_accessed=400_000_000, transcendentals=0),
-        name="gather_weights",
-    )(in_own[0], in_own[1], out_own)
+        name="front",
+    )(in_own, out_own, stream, gain.reshape(1, width), masks)
 
 
 def finish_kernel(x_ref, first_0, first_1, first_2, first_3, conv_ref, gated_ref, gate_ref, mask_ref, conv_weight,
@@ -843,7 +962,6 @@
 
 from jax.sharding import PartitionSpec as P
 
-EPSILON = 1e-05
 BF16 = jnp.bfloat16
 
 
@@ -906,9 +1024,7 @@
     modes, depth = in_weight.shape[:2]
     in_own = in_weight.transpose(2, 0, 1, 3)
     fast = (lax.axis_size("shard"), lax.axis_size("ctx"), lax.axis_size("tp")) == (4, 4, 2)
-    if fast:
-        conv_weight, gate_weight, full_out = gather_weights(in_own, out_weight)
-    else:
+    if not fast:
         conv_weight, gate_weight = lax.all_gather(in_own, "shard", axis=2, tiled=True)
         full_out = lax.all_gather(out_weight, "shard", axis=1, tiled=True)
     full_select = lax.all_gather(select_weight, "shard", axis=1, tiled=True)
@@ -942,15 +1058,22 @@
         return jnp.stack([product(values * masks[index], grads, 0, 0) for index in range(modes)])
 
     g_mix = lax.all_gather(upstream, "tp", axis=2, tiled=True).reshape(rows, width) * valid_rows.astype(BF16)
+
+    if fast:
+        conv_weight, gate_weight, full_out, conv_in, gate_in, normed, whole = front(
+            in_own, out_weight, stream.reshape(rows, part_width), norm_gain, masks_float[:, :, 0].T
+        )
+        whole = whole.astype(jnp.float32)
+    else:
+        whole = lax.all_gather(stream, "tp", axis=2, tiled=True).reshape(rows, width).astype(jnp.float32)
+    inverse = lax.rsqrt(jnp.mean(whole * whole, axis=1, keepdims=True) + EPSILON)
+    if not fast:
+        normed = (whole * inverse * norm_gain).astype(BF16)
+        normed_modes = jnp.concatenate([normed * masks[index] for index in range(modes)], axis=1)
+        conv_in = product(normed_modes, conv_weight.reshape(modes * width, inner), 1, 0).astype(BF16)
+        gate_in = product(normed_modes, gate_weight.reshape(modes * width, inner), 1, 0)
+    conv_in = conv_in.reshape(seqs, local_len, inner)
     g_gated = product(g_mix, full_out, 1, 1)
-
-    whole = lax.all_gather(stream, "tp", axis=2, tiled=True).reshape(rows, width).astype(jnp.float32)
-    inverse = lax.rsqrt(jnp.mean(whole * whole, axis=1, keepdims=True) + EPSILON)
-    normed = (whole * inverse * norm_gain).astype(BF16)
-    normed_modes = jnp.concatenate([normed * masks[index] for index in range(modes)], axis=1)
-    conv_in = product(normed_modes, conv_weight.reshape(modes * width, inner), 1, 0)
-    conv_in = conv_in.astype(BF16).reshape(seqs, local_len, inner)
-    gate_in = product(normed_modes, gate_weight.reshape(modes * width, inner), 1, 0)
 
     def terms_of(lefts, grads):
         return jnp.stack([product(left, grads, 1, 0) for left in lefts]).astype(BF16)

time: 755 us -> 708 us (0.938)
  matrix products: 75.7 us -> 49.7 us
  local copies, waits for them, and re-layouts: 77.9 us -> 63.8 us
    dot_general x20 -> x18, matrix products: 75.7 us -> 49.7 us  [product(): lax.dot_general(left, right, (((left_dim,), (right_dim,)), ((), ())), pre...]
    unnamed x167 -> x158, local copies, waits for them, and re-layouts: 41.6 us -> 32.3 us
  transfers between devices with their start and end apart: 18 -> 17, of which waited for: 1 -> 1; matrix products, arithmetic and copies ran while one was open for 25% -> 22% of each run, Pallas kernels for 51% -> 54%
where the time goes in v3:
time: 708 us; the launch traced here: 699 us
  Pallas kernels  483 us (68%)
  other arithmetic  64.9 us (9%)
  local copies, waits for them, and re-layouts  63.8 us (9%)
  matrix products  49.7 us (7%)
  between operations  21.6 us (3%)
  starting transfers between devices  12.1 us (2%)
    pallas_call x1, Pallas kernels, finish_weights(): pl.pallas_call(finish_kernel, in_specs=[vmem] + [any_space] * 7 + [vmem]...  158 us
    pallas_call x1, Pallas kernels, front(): pl.pallas_call(front_kernel, in_specs=[any_space] + [vmem] * 4, out_specs...  149 us
    pallas_call x2, Pallas kernels, scan_both(): pl.pallas_call(functools.partial(scan_kernel, groups, states, states, sta...  101 us
    pallas_call x1, Pallas kernels, scan_entering(): pl.pallas_call(functools.partial(entering_kernel, groups, states, seqs),...  52.8 us
    dot_general x18, matrix products, product(): lax.dot_general(left, right, (((left_dim,), (right_dim,)), ((), ())), pre...  49.7 us
    unnamed x158, local copies, waits for them, and re-layouts  32.3 us
    pallas_call x1, Pallas kernels, small_sum(): pl.pallas_call(small_kernel, in_specs=[vmem], out_specs=vmem, out_shape=j...  21.6 us
  transfers between devices with their start and end apart: 17, of which 1 were waited for; matrix products, arithmetic and copies ran while one was open for 22% of the time, Pallas kernels for 54%

profile of v3, /device:TPU:1, one launch (start us, length us, event | category | flops | bytes accessed | tf_op | source)
XLA Modules:
  0.0 699.0 jit_solution(3979083106039877516)
XLA Ops:
  10.3 10.6 %copy.110 = bf16[2,512,2,2048]{3,1,0,2:T(8,128)(2,1)} copy(bf16[2,512,2,2048]{3,2,1,0:T(2,128)(2,1)} %param.17) | data formatting | bytes 16777216 | tf_op args[2]
  20.9 149.2 %front.1 = (bf16[2,2048,2048]{2,1,0:T(8,128)(2,1)}, bf16[2,2048,2048]{2,1,0:T(8,128)(2,1)}, bf16[2048,2048]{1,0:T(8,128)(2,1)}, bf16[512,2048]{1,0:T(8,128)(2,1)...) custom-call(bf16[2,2,512,2048]{3,2,1,0:T(8,128)(2,1)} %bitcast.211, ...), custom_call_target="tpu_custom_call" | custom-call | bytes 400000000 | tf_op jit(solution)/shard_map/front/pallas_call | solution.py:586
  178.5 5.6 broadcast_multiply_fusion.1
  185.9 2.6 fusion.47
  188.5 2.6 convolution_add_fusion
  194.2 10.2 %fusion.79.gg_ref = f32[512,2048]{1,0:T(8,128)} fusion(bf16[512,2048]{1,0:T(8,128)(2,1)S(1)} %bitcast_multiply_fusion.gmix_ref, bf16[2048,2048]{1,0:T(8,128)(2,1)} %get-tuple-element.64), kind=kOutput, calls=%fused_computation.189 | convolution fusion | flops 4294967296 | bytes 14680064 | tf_op jit(solution)/shard_map/dot_general | solution.py:975
  208.1 3.1 add_add_fusion.raw_ref
  211.3 52.8 %scan_entering.1 = (f32[4,128,128]{2,1,0:T(8,128)}, f32[4,128,128]{2,1,0:T(8,128)}, bf16[2048,512]{1,0:T(8,128)(2,1)}, bf16[2048,512]{1,0:T(8,128)(2,1)}, bf16[16,2048]{1,0:T(8,128)(2,1)}) custom-call(f32[512,2048]{1,0:T(8,128)} %add_add_fusion.raw_ref, bf16[512,2048]{1,0:T(8,128)(2,1)} %bitcast.212, f32[512,2048]{1,0:T(8,128)} %get-tuple-element.63.gate_ref, ...), custom_call_target="tpu_custom_call" | custom-call | flops 134217728 | bytes 16777216 | tf_op jit(solution)/shard_map/scan_entering/pallas_call | solution.py:877
  267.5 50.2 %scan_both.2 = (bf16[512,1024]{1,0:T(8,128)(2,1)}, bf16[512,1024]{1,0:T(8,128)(2,1)}, bf16[512,1024]{1,0:T(8,128)(2,1)}, f32[512,1024]{1,0:T(8,128)}, f32[2,16,8...) custom-call(f32[512,2048]{1,0:T(8,128)} %add_add_fusion.raw_ref, ...), custom_call_target="tpu_custom_call" | custom-call | flops 184549376 | bytes 16777216 | tf_op jit(solution)/shard_map/scan_both/pallas_call | solution.py:364
  322.1 50.4 %scan_both.3 = (bf16[512,1024]{1,0:T(8,128)(2,1)}, bf16[512,1024]{1,0:T(8,128)(2,1)}, bf16[512,1024]{1,0:T(8,128)(2,1)}, f32[512,1024]{1,0:T(8,128)}, f32[2,16,8...) custom-call(f32[512,2048]{1,0:T(8,128)} %add_add_fusion.raw_ref, ...), custom_call_target="tpu_custom_call" | custom-call | flops 184549376 | bytes 16777216 | tf_op jit(solution)/shard_map/scan_both/pallas_call | solution.py:364
  374.8 2.9 copy.82
  377.7 4.0 copy.84
  383.3 3.2 pad_maximum_fusion.x_ref
  386.5 4.7 fusion.37
  397.2 5.5 fusion.33
  414.8 7.2 %fusion.15 = f32[512,2048]{1,0:T(8,128)S(1)} fusion(bf16[2048,2048]{1,0:T(8,128)(2,1)} %get-tuple-element.64, bf16[512,1024]{1,0:T(8,128)(2,1)} %get-tuple-element.88.gated_ref, bf16[512,1024]{1,0:T(8,128)(2,1)S(1)} %copy-done.28), kind=kOutput, calls=%fused_computation.46 | convolution fusion | flops 4299161600 | bytes 14680064 | tf_op jit(solution)/shard_map/dot_general | solution.py:975
  439.5 4.2 multiply_reduce_fusion
  453.8 10.6 %pad_add_fusion = f32[2,259,2048]{2,1,0:T(8,128)} fusion(f32[2,256,2048]{2,1,0:T(8,128)} %copy-done.2, f32[2,256,2048]{2,1,0:T(8,128)} %copy-done.3, f32[2,256,2048]{2,1,0:T(8,128)} %copy-done.4, f32[2,256,2048]{2,1,0:T(8,128)} %copy-done.1), kind=kLoop, calls=%fused_computation.5 | loop fusion | flops 3182592 | bytes 21020672 | tf_op jit(solution)/shard_map/add | solution.py:1168
  468.8 4.1 fusion.4
  473.0 158.5 %finish_weights.1 = (f32[14,128,512]{2,1,0:T(8,128)}, f32[512,2048]{1,0:T(8,128)}, bf16[512,1024]{1,0:T(8,128)(2,1)}) custom-call(bf16[3,512,2048]{2,1,0:T(8,128)(2,1)} %pad_maximum_fusion.x_ref, bf16[512,1024]{1,0:T(8,128)(2,1)} %get-tuple-element.80.first_0, bf16[512,1024]{1,0:T(8,128)(2,1)} %collective-permute-done.3.first_1, ...), custom_call_target="tpu_custom_call" | custom-call | flops 49392123904 | bytes 500000000 | tf_op jit(solution)/shard_map/finish_weights/pallas_call | solution.py:840
  631.5 3.6 fusion.3
  642.4 4.5 multiply_reduce_fusion.4
  647.9 21.6 %small_sum.1 = f32[32,2048]{1,0:T(8,128)S(1)} custom-call(f32[32,2048]{1,0:T(8,128)S(1)} %concatenate.68.in_ref), custom_call_target="tpu_custom_call" | custom-call | bytes 40000000 | tf_op jit(solution)/shard_map/small_sum/pallas_call | solution.py:949
  681.7 5.3 copy.92
  (301 shorter events, 100.2 us)
Async XLA Ops:
  7.2 178.8 %all-gather.6.cloned.1.call-start = ((), (), s32[]{:S(2)}) async-start(), calls=%async_computation.3 | async-start | bytes 1638400 | tf_op jit(solution)/shard_map/all_gather | solution.py:1030
  7.9 184.5 %all-gather.10.cloned.1.call-start = ((), (), s32[]{:S(2)}) async-start(), calls=%async_computation.5 | async-start | bytes 3145728 | tf_op jit(solution)/shard_map/all_gather | solution.py:1060
  8.7 197.6 %all-gather.8.cloned.1.call-start = ((), (), s32[]{:S(2)}) async-start(), calls=%async_computation.4 | async-start | bytes 1310720 | tf_op jit(solution)/shard_map/all_gather | solution.py:1031
  20.9 153.1 %copy-start.46 = (f32[4,2048]{1,0:T(4,128)S(1)}, f32[4,2048]{1,0:T(4,128)}, u32[]{:S(2)}) copy-start(f32[4,2048]{1,0:T(4,128)} %param.22) | copy-start | bytes 98308
  20.9 153.3 %copy-start.66 = (f32[2,2048]{1,0:T(2,128)S(1)}, f32[2,2048]{1,0:T(2,128)}, u32[]{:S(2)}) copy-start(f32[2,2048]{1,0:T(2,128)} %param.20) | copy-start | bytes 49156
  20.9 153.3 %copy-start.69 = (s32[2,256]{1,0:T(2,128)S(1)}, s32[2,256]{1,0:T(2,128)}, u32[]{:S(2)}) copy-start(s32[2,256]{1,0:T(2,128)} %param.28) | copy-start | bytes 6148
  20.9 153.3 %copy-start.33 = (f32[16,2048]{1,0:T(8,128)S(1)}, f32[16,2048]{1,0:T(8,128)}, u32[]{:S(2)}) copy-start(f32[16,2048]{1,0:T(8,128)} %param.24) | copy-start | bytes 393220
  171.0 5.2 collective-permute-start
  173.2 213.3 %all-gather.12.cloned.1.call-start = ((), (), s32[]{:S(2)}) async-start(), calls=%async_computation.6 | async-start | bytes 5242880 | tf_op jit(solution)/shard_map/all_gather | solution.py:1130
  191.1 13.3 %collective-permute-start.1 = (f32[512,160]{0,1:T(8,128)S(1)}, f32[512,160]{0,1:T(8,128)S(1)}, u32[]{:S(2)}, u32[]{:S(2)}) collective-permute-start(f32[512,160]{0,1:T(8,128)S(1)} %convolution_add_fusion), channel_id=1, source_target_pairs={{0,1},{1,0},{2,3},{3,2},{4,5},{5,4},{6,7},{7,6},{8,9},{9,8},{10,11... | collective-permute-start | bytes 983048 | tf_op jit(solution)/shard_map/ppermute | solution.py:1047
  317.7 79.5 %all-gather.14.cloned.1.call-start = ((), (), s32[]{:S(2)}) async-start(), calls=%async_computation.7 | async-start | bytes 5242880 | tf_op jit(solution)/shard_map/all_gather | solution.py:1131
  318.3 357.0 %reduce-scatter.8.cloned.1.call-start = ((), (), s32[]{:S(2)}) async-start(), calls=%async_computation.10 | async-start | bytes 1310720 | tf_op jit(solution)/shard_map/reduce_scatter | solution.py:1082
  372.6 100.3 %collective-permute-start.3 = (bf16[512,1024]{1,0:T(8,128)(2,1)}, bf16[512,1024]{1,0:T(8,128)(2,1)}, u32[]{:S(2)}, u32[]{:S(2)}) collective-permute-start(bf16[512,1024]{1,0:T(8,128)(2,1)} %get-tuple-element.80.first_0), channel_id=1, source_target_pairs={{0,8},{8,0},{16,24},{24,16},{1,9},{9,1},{17,25},{25,17},{2,10},{10... | collective-permute-start | bytes 3145736 | tf_op jit(solution)/shard_map/ppermute | solution.py:1135
  372.7 100.2 %collective-permute-start.4 = (bf16[512,1024]{1,0:T(8,128)(2,1)}, bf16[512,1024]{1,0:T(8,128)(2,1)}, u32[]{:S(2)}, u32[]{:S(2)}) collective-permute-start(bf16[512,1024]{1,0:T(8,128)(2,1)} %get-tuple-element.80.first_0), channel_id=1, source_target_pairs={{0,16},{8,24},{16,0},{24,8},{1,17},{9,25},{17,1},{25,9},{2,18},{10... | collective-permute-start | bytes 3145736 | tf_op jit(solution)/shard_map/ppermute | solution.py:1135
  374.1 98.8 %collective-permute-start.5 = (bf16[512,1024]{1,0:T(8,128)(2,1)}, bf16[512,1024]{1,0:T(8,128)(2,1)}, u32[]{:S(2)}, u32[]{:S(2)}) collective-permute-start(bf16[512,1024]{1,0:T(8,128)(2,1)} %get-tuple-element.80.first_0), channel_id=1, source_target_pairs={{0,24},{8,16},{16,8},{24,0},{1,25},{9,17},{17,9},{25,1},{2,26},{10... | collective-permute-start | bytes 3145736 | tf_op jit(solution)/shard_map/ppermute | solution.py:1135
  412.1 21.6 %collective-permute-start.6 = (f32[512,160]{0,1:T(8,128)}, f32[512,160]{0,1:T(8,128)}, u32[]{:S(2)}, u32[]{:S(2)}) collective-permute-start(f32[512,160]{0,1:T(8,128)} %pad_maximum_fusion.3), channel_id=1, source_target_pairs={{0,1},{1,0},{2,3},{3,2},{4,5},{5,4},{6,7},{7,6},{8,9},{9,8},{10,11... | collective-permute-start | bytes 983048 | tf_op jit(solution)/shard_map/ppermute | solution.py:1047
  414.5 264.2 %reduce-scatter.4.cloned.1.call-start = ((), (), s32[]{:S(2)}) async-start(), calls=%async_computation.8 | async-start | bytes 2621440 | tf_op jit(solution)/shard_map/reduce_scatter | solution.py:1082
  425.1 214.9 %collective-permute-start.2 = (bf16[512,1024]{1,0:T(8,128)(2,1)}, bf16[512,1024]{1,0:T(8,128)(2,1)}, u32[]{:S(2)}, u32[]{:S(2)}) collective-permute-start(bf16[512,1024]{1,0:T(8,128)(2,1)} %dynamic-slice_convert_fusion), channel_id=1, source_target_pairs={{0,1},{1,0},{2,3},{3,2},{4,5},{5,4},{6,7},{7,6},{8,9},{9,8},{10,11... | collective-permute-start | bytes 3145736 | tf_op jit(solution)/shard_map/ppermute | solution.py:1054
  430.2 256.8 %reduce-scatter.6.cloned.1.call-start = ((), (), s32[]{:S(2)}) async-start(), calls=%async_computation.9 | async-start | bytes 3342336 | tf_op jit(solution)/shard_map/reduce_scatter | solution.py:1196
  451.7 17.1 %collective-permute-start.7 = (f32[2,3,2048]{2,1,0:T(4,128)S(1)}, f32[2,3,2048]{2,1,0:T(4,128)S(1)}, u32[]{:S(2)}, u32[]{:S(2)}) collective-permute-start(f32[2,3,2048]{2,1,0:T(4,128)S(1)} %pad_add_fusion.1), channel_id=1, source_target_pairs={{2,0},{4,2},{6,4},{3,1},{5,3},{7,5},{10,8},{12,10},{14,12},{11,9},... | collective-permute-start | bytes 147464 | tf_op jit(solution)/shard_map/ppermute | solution.py:971
  472.9 158.5 %copy-start.10 = (bf16[512,2048]{1,0:T(8,128)(2,1)S(1)}, bf16[512,2048]{1,0:T(8,128)(2,1)}, u32[]{:S(2)}) copy-start(bf16[512,2048]{1,0:T(8,128)(2,1)} %get-tuple-element.89) | copy-start | bytes 6291460
  472.9 158.5 %copy-start.44 = (f32[2048]{0:T(1024)S(1)}, f32[2048]{0:T(1024)}, u32[]{:S(2)}) copy-start(f32[2048]{0:T(1024)} %param.16) | copy-start | bytes 24580
  472.9 158.5 %copy-start.60 = (f32[512]{0:T(512)S(1)}, f32[512]{0:T(512)}, u32[]{:S(2)}) copy-start(f32[512]{0:T(512)} %get-tuple-element.237) | copy-start | bytes 6148
  635.1 4.9 collective-permute-start.8
  (66 other events, 671.4 us)
Sparse Core Ops, SparseCore 0:
  9.6 23.5 all-gather.5
  34.7 37.9 all-gather.9
  173.4 16.1 all-gather.7
  317.8 33.5 all-gather.11
  352.8 44.3 all-gather.13
  414.6 26.9 reduce-scatter.7
  444.0 43.8 reduce-scatter.3
  491.8 84.0 reduce-scatter.5
